TPU v7x, 128 devices: a whole 4x4x4 slice. The times are simulated.
128 devices in a mesh: row: 4 (over x), col: 32 (over z, y, core).
Axes of the slice: x: 4, y: 4, z: 4, core: 2. Of those that a mesh axis runs over, the one named last changes fastest.
Arguments:
- tokens: bfloat16 [512, 8192], P('col', 'row'), may hold values from -6 to 6
- out_grad: bfloat16 [512, 8192], P('col', 'row'), may hold values from -6 to 6
- gate_weight: bfloat16 [8192, 29568], P('row', 'col'), may hold values from -0.0625 to 0.0625
- up_weight: bfloat16 [8192, 29568], P('row', 'col'), may hold values from -0.0625 to 0.0625
- down_weight: bfloat16 [29568, 8192], P('col', 'row'), may hold values from -0.03125 to 0.03125
Outputs:
- input_grad: bfloat16 [512, 8192], P('col', 'row')
- gate_wgrad: bfloat16 [8192, 29568], P('row', 'col')
- up_wgrad: bfloat16 [8192, 29568], P('row', 'col')
- down_wgrad: bfloat16 [29568, 8192], P('col', 'row')
All inputs are finite; a program needn't handle non-finite values.
Results may differ from a plain program's by a relative error of at most 0.005.
Values may be sent and summed in bfloat16 or wider, within the bound.
No kernel may reach another device: no remote copies, remote signals or barrier semaphores. Data moves between devices by JAX's collectives and lax.ppermute only.
A program may use at most 128 MiB of HBM per device.

v0:
```python
import math

import jax
import jax.numpy as jnp
from jax import lax
from jax.sharding import PartitionSpec as P


def contract(left, right, left_dim, right_dim):
    return lax.dot_general(
        left, right, (((left_dim,), (right_dim,)), ((), ())), preferred_element_type=jnp.float32
    )


def swiglu_backward(gate, upward, hid_grad):
    sig = jax.nn.sigmoid(gate)
    act = gate * sig
    hidden = (act * upward).astype(jnp.bfloat16)
    gate_grad = (hid_grad * upward * sig * (1.0 + gate * (1.0 - sig))).astype(jnp.bfloat16)
    up_grad = (hid_grad * act).astype(jnp.bfloat16)
    return (hidden, gate_grad, up_grad)


def local(tokens, out_grad, gate_weight, up_weight, down_weight):
    panel_tokens, panel_grads = (
        lax.all_gather(tokens, "col", axis=0, tiled=True),
        lax.all_gather(out_grad, "col", axis=0, tiled=True),
    )
    factor = 1.0 / math.sqrt(panel_tokens.shape[0])
    gate_part = jnp.dot(panel_tokens, gate_weight, preferred_element_type=jnp.float32)
    up_part = jnp.dot(panel_tokens, up_weight, preferred_element_type=jnp.float32)
    grad_part = contract(panel_grads, down_weight, 1, 1)
    gate, upward, hid_grad = lax.psum((gate_part, up_part, grad_part), "row")
    hidden, gate_grad, up_grad = swiglu_backward(gate, upward, hid_grad)
    input_grad = lax.psum_scatter(
        contract(gate_grad, gate_weight, 1, 1) + contract(up_grad, up_weight, 1, 1),
        "col",
        scatter_dimension=0,
        tiled=True,
    ).astype(jnp.bfloat16)
    gate_wgrad = (contract(panel_tokens, gate_grad, 0, 0) * factor).astype(jnp.bfloat16)
    up_wgrad = (contract(panel_tokens, up_grad, 0, 0) * factor).astype(jnp.bfloat16)
    down_wgrad = (contract(hidden, panel_grads, 0, 0) * factor).astype(jnp.bfloat16)
    return (input_grad, gate_wgrad, up_wgrad, down_wgrad)


def solution(mesh):
    placed = (P("col", "row"), P("col", "row"), P("row", "col"), P("row", "col"), P("col", "row"))
    return jax.shard_map(
        local,
        mesh=mesh,
        in_specs=placed,
        out_specs=(P("col", "row"), P("row", "col"), P("row", "col"), P("col", "row")),
        check_vma=False,
    )
```

profile of v0, /device:TPU:1, one launch (start us, length us, event | category | flops | bytes accessed | tf_op | source)
XLA Modules:
  0.0 325.7 jit_solution(14472059379591102396)
XLA Ops:
  7.2 0.0 all-gather.5.cloned.1.call-start
  7.2 0.7 all-gather.5.cloned.1.call-update
  7.9 0.0 all-gather.3.cloned.1.call-start
  7.9 0.7 all-gather.3.cloned.1.call-update
  8.6 0.0 all-reduce.3.cloned.1.call-start
  8.7 49.2 %all-gather.5.cloned.1.call-done = bf16[512,2048]{1,0:T(8,128)(2,1)} async-done(((bf16[16,2048]{1,0:T(8,128)(2,1)}), bf16[512,2048]{1,0:T(8,128)(2,1)}) %all-gather.5.cloned.1.call-update) | async-done | bytes 2097168 | tf_op jit(solution)/shard_map/all_gather | solution.py:26
  57.9 0.0 copy-start
  57.9 0.0 copy-start.5
  57.9 6.3 %fusion.6 = f32[512,924]{0,1:T(8,128)} fusion(bf16[512,2048]{1,0:T(8,128)(2,1)} %all-gather.5.cloned.1.call-done, bf16[2048,924]{0,1:T(8,128)(2,1)} %param.8), kind=kOutput, calls=%fused_computation.13 | convolution fusion | flops 1937768448 | bytes 7774208 | tf_op jit(solution)/shard_map/dot_general | solution.py:31
  64.2 0.0 copy-done
  64.2 0.0 copy-done.5
  64.2 3.4 %fusion.7 = f32[512,924]{0,1:T(8,128)} fusion(bf16[512,2048]{1,0:T(8,128)(2,1)S(1)} %copy-done.5, bf16[2048,924]{0,1:T(8,128)(2,1)S(1)} %copy-done), kind=kOutput, calls=%fused_computation.14 | convolution fusion | flops 1937768448 | bytes 7774208 | tf_op jit(solution)/shard_map/dot_general | solution.py:30
  67.6 35.8 %all-gather.3.cloned.1.call-done = bf16[512,2048]{1,0:T(8,128)(2,1)} async-done(((bf16[16,2048]{1,0:T(8,128)(2,1)}), bf16[512,2048]{1,0:T(8,128)(2,1)}) %all-gather.3.cloned.1.call-update) | async-done | bytes 2097168 | tf_op jit(solution)/shard_map/all_gather | solution.py:27
  103.5 6.1 %fusion.5 = f32[512,924]{0,1:T(8,128)} fusion(bf16[512,2048]{1,0:T(8,128)(2,1)} %all-gather.3.cloned.1.call-done, bf16[924,2048]{1,0:T(8,128)(2,1)} %param.9), kind=kOutput, calls=%fused_computation.12 | convolution fusion | flops 1937768448 | bytes 7774208 | tf_op jit(solution)/shard_map/dot_general | solution.py:10
  109.6 0.0 all-reduce.3.cloned.1.call-update
  109.6 0.2 reduce-scatter.2.cloned.1.call-start
  109.8 116.3 %all-reduce.3.cloned.1.call-done = (f32[512,924]{0,1:T(8,128)}, f32[512,924]{0,1:T(8,128)}, f32[512,924]{0,1:T(8,128)}) async-done(((f32[512,924]{0,1:T(8,128)}, f32[512,924]{0,1:T(8,128)}, f32[512,924]{0,1:T(8,128)}), (f32[512,924]{0,1:T(8,128)}, f32[512,924]{0,1:T(8,128)}, f32[512,924]{0,1:T(8,128)})) %all-reduce.3.cloned.1.call-update) | async-done | bytes 5677072 | tf_op jit(solution)/shard_map/psum | solution.py:33
  226.1 0.0 copy-start.1
  226.1 3.9 %multiply_convert_fusion.4 = (bf16[512,924]{0,1:T(8,128)(2,1)S(1)}, bf16[512,924]{0,1:T(8,128)(2,1)S(1)}) fusion(f32[512,924]{0,1:T(8,128)} %get-tuple-element.5, f32[512,924]{0,1:T(8,128)} %get-tuple-element.4, f32[512,924]{0,1:T(8,128)} %get-tuple-element.6), kind=kLoop, calls=%fused_computation.7 | loop fusion | flops 6150144 | bytes 7569408 | tf_op jit(solution)/shard_map/convert_element_type | solution.py:20
  230.0 0.0 copy-done.1
  230.0 0.0 copy-start.2
  230.0 2.4 fusion.8
  232.5 0.0 copy-done.2
  232.5 4.5 %convolution_add_fusion = f32[512,2048]{1,0:T(8,128)} fusion(f32[512,2048]{1,0:T(8,128)S(1)} %fusion.8, bf16[512,924]{0,1:T(8,128)(2,1)S(1)} %get-tuple-element.7, bf16[2048,924]{0,1:T(8,128)(2,1)S(1)} %copy-done.2), kind=kOutput, calls=%fused_computation.5 | convolution fusion | flops 1938817024 | bytes 13119488 | tf_op jit(solution)/shard_map/dot_general | solution.py:10
  237.0 0.0 reduce-scatter.2.cloned.1.call-update
  237.0 0.0 copy-start.6
  237.0 5.8 %fusion = bf16[2048,924]{0,1:T(8,128)(2,1)} fusion(bf16[512,924]{0,1:T(8,128)(2,1)S(1)} %get-tuple-element.8, bf16[512,2048]{1,0:T(8,128)(2,1)} %all-gather.5.cloned.1.call-done), kind=kOutput, calls=%fused_computation.3 | convolution fusion | flops 1941553152 | bytes 6828032 | tf_op jit(solution)/shard_map/dot_general | solution.py:10
  242.8 0.0 copy-done.6
  242.8 0.0 copy-start.3
  242.8 0.0 copy-start.4
  242.8 0.0 copy-start.7
  242.8 4.1 %fusion.1 = bf16[2048,924]{0,1:T(8,128)(2,1)} fusion(bf16[512,924]{0,1:T(8,128)(2,1)S(1)} %get-tuple-element.7, bf16[512,2048]{1,0:T(8,128)(2,1)S(1)} %copy-done.6), kind=kOutput, calls=%fused_computation.4 | convolution fusion | flops 1941553152 | bytes 6828032 | tf_op jit(solution)/shard_map/dot_general | solution.py:10
  246.9 0.0 copy-done.3
  246.9 0.0 copy-done.4
  246.9 0.0 copy-done.7
  246.9 4.1 %multiply_convert_fusion = bf16[924,2048]{1,0:T(8,128)(2,1)} fusion(bf16[512,2048]{1,0:T(8,128)(2,1)S(1)} %copy-done.7, f32[512,924]{0,1:T(8,128)S(1)} %copy-done.4, f32[512,924]{0,1:T(8,128)S(1)} %copy-done.3), kind=kOutput, calls=%fused_computation | convolution fusion | flops 1944391680 | bytes 9666560 | tf_op jit(solution)/shard_map/dot_general | solution.py:10
  251.0 66.6 %reduce-scatter.2.cloned.1.call-done = f32[16,2048]{1,0:T(8,128)} async-done(((f32[512,2048]{1,0:T(8,128)}), f32[16,2048]{1,0:T(8,128)}) %reduce-scatter.2.cloned.1.call-update) | async-done | bytes 131088 | tf_op jit(solution)/shard_map/reduce_scatter | solution.py:35
  317.6 1.5 convert_element_type.29
Async XLA Ops:
  7.2 50.8 %all-gather.5.cloned.1.call-start = ((), (), s32[]{:S(2)}) async-start(), calls=%async_computation.2 | async-start | bytes 2162688 | tf_op jit(solution)/shard_map/all_gather | solution.py:26
  7.9 95.6 %all-gather.3.cloned.1.call-start = ((), (), s32[]{:S(2)}) async-start(), calls=%async_computation.1 | async-start | bytes 2162688 | tf_op jit(solution)/shard_map/all_gather | solution.py:27
  8.6 217.5 %all-reduce.3.cloned.1.call-start = ((), (), s32[]{:S(2)}) async-start(), calls=%async_computation.4 | async-start | bytes 11403264 | tf_op jit(solution)/shard_map/psum | solution.py:33
  57.9 6.3 %copy-start = (bf16[2048,924]{0,1:T(8,128)(2,1)S(1)}, bf16[2048,924]{0,1:T(8,128)(2,1)}, u32[]{:S(2)}) copy-start(bf16[2048,924]{0,1:T(8,128)(2,1)} %param.7) | copy-start | bytes 11354116
  57.9 6.3 %copy-start.5 = (bf16[512,2048]{1,0:T(8,128)(2,1)S(1)}, bf16[512,2048]{1,0:T(8,128)(2,1)}, u32[]{:S(2)}) copy-start(bf16[512,2048]{1,0:T(8,128)(2,1)} %all-gather.5.cloned.1.call-done) | copy-start | bytes 6291460
  109.6 208.0 %reduce-scatter.2.cloned.1.call-start = ((), (), s32[]{:S(2)}) async-start(), calls=%async_computation.3 | async-start | bytes 4325376 | tf_op jit(solution)/shard_map/reduce_scatter | solution.py:35
  226.1 3.9 %copy-start.1 = (bf16[2048,924]{0,1:T(8,128)(2,1)S(1)}, bf16[2048,924]{0,1:T(8,128)(2,1)}, u32[]{:S(2)}) copy-start(bf16[2048,924]{0,1:T(8,128)(2,1)} %param.7) | copy-start | bytes 11354116
  230.0 2.4 copy-start.2
  237.0 5.8 %copy-start.6 = (bf16[512,2048]{1,0:T(8,128)(2,1)S(1)}, bf16[512,2048]{1,0:T(8,128)(2,1)}, u32[]{:S(2)}) copy-start(bf16[512,2048]{1,0:T(8,128)(2,1)} %all-gather.5.cloned.1.call-done) | copy-start | bytes 6291460
  242.8 4.1 %copy-start.3 = (f32[512,924]{0,1:T(8,128)S(1)}, f32[512,924]{0,1:T(8,128)}, u32[]{:S(2)}) copy-start(f32[512,924]{0,1:T(8,128)} %get-tuple-element.4) | copy-start | bytes 5677060
  242.8 4.1 %copy-start.4 = (f32[512,924]{0,1:T(8,128)S(1)}, f32[512,924]{0,1:T(8,128)}, u32[]{:S(2)}) copy-start(f32[512,924]{0,1:T(8,128)} %get-tuple-element.6) | copy-start | bytes 5677060
  242.8 4.1 %copy-start.7 = (bf16[512,2048]{1,0:T(8,128)(2,1)S(1)}, bf16[512,2048]{1,0:T(8,128)(2,1)}, u32[]{:S(2)}) copy-start(bf16[512,2048]{1,0:T(8,128)(2,1)} %all-gather.3.cloned.1.call-done) | copy-start | bytes 6291460
Sparse Core Ops, SparseCore 0:
  10.3 47.6 all-gather.4
  60.2 43.2 all-gather.2
  109.7 116.3 all-reduce.2
  237.1 80.4 reduce-scatter.1
where the time goes:
time: 327 us; the launch traced here: 326 us
  waiting for transfers between devices  269 us (82%)
  matrix products  36.7 us (11%)
  between operations  13.8 us (4%)
  other arithmetic  5.43 us (2%)
    psum x1, waiting for transfers between devices, local(): gate, upward, hid_grad = lax.psum((gate_part, up_part, grad_part), 'row')  116 us
    reduce_scatter x1, waiting for transfers between devices, local(): lax.psum_scatter(contract(gate_grad, gate_weight, 1, 1) + contract(up_gra...  66.6 us
    all_gather x1, waiting for transfers between devices, local(): lax.all_gather(tokens, 'col', axis=0, tiled=True)  49.2 us
    all_gather x1, waiting for transfers between devices, local(): lax.all_gather(out_grad, 'col', axis=0, tiled=True)  35.8 us
    dot_general x6, matrix products, contract(): lax.dot_general(left, right, (((left_dim,), (right_dim,)), ((), ())), pre...  27 us
  transfers between devices with their start and end apart: 4, of which 4 were waited for; matrix products, arithmetic and copies ran while one was open for 7% of the time, Pallas kernels for 0%

commit v1 on v0

v1 whole, which is shorter than its diff:
```python
import functools
import math

import jax
import jax.numpy as jnp
from jax import lax
from jax.experimental import pallas as pl
from jax.experimental.pallas import tpu as pltpu
from jax.sharding import PartitionSpec as P

BF16 = jnp.bfloat16
F32 = jnp.float32
ROWS, PLANES, LINES, CORES = 4, 4, 4, 2
FLIP = (0, 2, 1, 3)
MAIN, TAIL, STEP, LANES = 896, 28, 32, 128
PACKED = 3 * MAIN + LANES
TILES = ((0, 256), (256, 256), (512, 256), (768, 128))
VMEM = pl.BlockSpec(memory_space=pltpu.VMEM)
SMEM = pl.BlockSpec(memory_space=pltpu.SMEM)


def device(x, z, y, c):
    return ((x % ROWS) * PLANES + z % PLANES) * LINES * CORES + (y % LINES) * CORES + c


def send(value, target):
    pairs = [
        (device(x, z, y, c), device(*target(x, z, y, c, 1 - 2 * c)))
        for x in range(ROWS)
        for z in range(PLANES)
        for y in range(LINES)
        for c in range(CORES)
    ]
    return lax.ppermute(value, ("row", "col"), pairs)


def swap_cores(value):
    return send(value, lambda x, z, y, c, w: (x, z, y, 1 - c))


def flip(value):
    return jnp.stack([value[i] for i in FLIP])


def after(value, *others):
    return lax.optimization_barrier((value, others))[0]


def call(kernel, outs, specs, scratch, cost, name):
    return pl.pallas_call(
        kernel,
        out_shape=[jax.ShapeDtypeStruct(s, t) for s, t in outs],
        in_specs=specs,
        out_specs=[VMEM] * len(outs),
        scratch_shapes=scratch,
        compiler_params=pltpu.CompilerParams(vmem_limit_bytes=40 * 2**20),
        cost_estimate=pl.CostEstimate(flops=cost[0], bytes_accessed=cost[1], transcendentals=0),
        name=name,
    )


def dot(left, right, dims):
    return lax.dot_general(left, right, (dims, ((), ())), preferred_element_type=F32)


def forward_kernel(layout, count, at, gate_w, up_w, down_w, tail_x, tail_g, *refs):
    sources, refs = refs[: layout[0]], refs[layout[0] :]
    x_ref, g_ref, far, near, relay, own, part = refs
    for row, (source, index) in enumerate(layout[1]):
        x_ref[row * 16 : row * 16 + 16] = sources[source][(*index, 0)]
        g_ref[row * 16 : row * 16 + 16] = sources[source][(*index, 1)]
    tails = dot(x_ref[...], tail_x[...], ((1,), (1,))) + dot(g_ref[...], tail_g[...], ((1,), (1,)))
    part[:, :, 3 * MAIN :] = tails.reshape(4, count, LANES)
    for i in range(3):
        rows, weight = (x_ref, x_ref, g_ref)[i], (gate_w, up_w, down_w)[i]
        for start, size in TILES:
            product = dot(weight[start : start + size], rows[...], ((1,), (1,))).T
            part[:, :, i * MAIN + start : i * MAIN + start + size] = product.reshape(4, count, size)
    own[...] = part[at[0]]
    near[...] = part[at[1]].astype(BF16)
    relay[...] = part[at[2]]
    far[...] = part[at[3]].astype(BF16)


def forward(at, weights, tails, sources, layout):
    rows = len(layout) * 16
    count, depth = rows // 4, tails[0].shape[1]
    kernel = functools.partial(forward_kernel, (len(sources), layout), count)
    return call(
        kernel,
        [((rows, depth), BF16)] * 2
        + [((count, PACKED), BF16)] * 2
        + [((count, PACKED), F32)] * 2,
        [SMEM] + [VMEM] * (5 + len(sources)),
        [pltpu.VMEM((4, count, PACKED), F32)],
        (6 * rows * depth * (MAIN + TAIL), 6 * MAIN * depth),
        "forward_products",
    )(at, *weights, tails[0], tails[1], *sources)


def swiglu_backward(gate, upward, hid_grad):
    sig = 1.0 / (1.0 + jnp.exp(-gate))
    act = gate * sig
    return (
        act * upward,
        hid_grad * upward * sig * (1.0 + gate * (1.0 - sig)),
        hid_grad * act,
    )


def activation_kernel(own, near, relay, mine):
    def whole(start, size):
        cut = slice(start, start + size)
        return own[:, cut] + near[:, cut].astype(F32) + relay[:, cut].astype(F32)

    for start in range(0, MAIN, LANES):
        parts = swiglu_backward(*(whole(i * MAIN + start, LANES) for i in range(3)))
        for i, v in enumerate(parts):
            mine[:, i * MAIN + start : i * MAIN + start + LANES] = v.astype(BF16)
    gate = whole(3 * MAIN, LANES)
    hidden, gate_grad, up_grad = swiglu_backward(
        gate, pltpu.roll(gate, LANES - STEP, 1), pltpu.roll(gate, LANES - 2 * STEP, 1)
    )
    lane = lax.broadcasted_iota(jnp.int32, gate.shape, 1)
    tail = jnp.where(lane < 2 * STEP, pltpu.roll(gate_grad, STEP, 1), pltpu.roll(up_grad, 2 * STEP, 1))
    tail = jnp.where(lane < STEP, hidden, tail)
    mine[:, 3 * MAIN :] = jnp.where(lane < 3 * STEP, tail, 0.0).astype(BF16)


def activation(own, near, relay):
    return call(
        activation_kernel,
        [(near.shape, BF16)],
        [VMEM] * 3,
        [],
        (20 * own.size, 10 * own.size),
        "activation",
    )(own, near, relay)[0]


def input_kernel(planes, at, gate_w, up_w, tail, mine, behind, ahead, across, q, keep, away):
    count = mine.shape[0]
    for i, v in enumerate((mine, behind, ahead, across)):
        q[at[i]] = v[...]
    def rows(start, size):
        return q[:, :, start : start + size].reshape(4 * count, size)

    for start in range(0, tail.shape[1], 512):
        cut = slice(start, start + 512)
        grad = (
            dot(rows(MAIN, MAIN), gate_w[:MAIN, cut], ((1,), (0,)))
            + dot(rows(2 * MAIN, MAIN), up_w[:MAIN, cut], ((1,), (0,)))
            + dot(rows(3 * MAIN, LANES), tail[:, cut], ((1,), (0,)))
        )
        for line in range(4):
            first = line * count
            if planes == 1:
                keep[line, :, cut] = grad[first : first + 16]
                away[FLIP[line], :, cut] = grad[first + 16 : first + 32]
            else:
                keep[line, 0, :, cut] = grad[first : first + 16]
                keep[line, 1, :, cut] = grad[first + 16 : first + 32]
                away[FLIP[line], 1, :, cut] = grad[first + 32 : first + 48]
                away[FLIP[line], 0, :, cut] = grad[first + 48 : first + 64]


def input_gradient(at, weights, tail, pieces):
    count, depth = pieces[0].shape[0], tail.shape[1]
    planes = count // 32
    part = (4, 16, depth) if planes == 1 else (4, 2, 16, depth)
    return call(
        functools.partial(input_kernel, planes),
        [((4, count, PACKED), BF16), (part, F32), (part, F32)],
        [SMEM] + [VMEM] * 7,
        [],
        (16 * count * depth * (MAIN + TAIL), 4 * MAIN * depth),
        "input_products",
    )(at, weights[0], weights[1], tail, *pieces)


def weight_kernel(factor, x, g, *refs):
    chunks, (gate_out, up_out, down_out, turned) = refs[:-4], refs[-4:]

    @pl.when(pl.program_id(0) == 0)
    def _():
        first = 0
        for q in chunks:
            rows = q.shape[0]
            for start in range(0, PACKED, LANES):
                turned[start : start + LANES, first : first + rows] = q[:, start : start + LANES].T
            first += rows

    x_tail = dot(turned[3 * MAIN :], x[...], ((1,), (0,))) * factor
    g_tail = dot(turned[3 * MAIN :], g[...], ((1,), (0,))) * factor
    for i, (out, rows, tail) in enumerate(((down_out, g, g_tail), (gate_out, x, x_tail), (up_out, x, x_tail))):
        product = dot(turned[i * MAIN : (i + 1) * MAIN], rows[...], ((1,), (0,))) * factor
        out[:MAIN] = product.astype(BF16)
        out[MAIN:] = tail[i * STEP : i * STEP + TAIL].astype(BF16)


def weight_gradients(x, g, chunks, factor):
    tokens, depth = x.shape
    width = 256
    column = pl.BlockSpec((tokens, width), lambda i: (0, i))
    out = pl.BlockSpec((MAIN + TAIL, width), lambda i: (0, i))
    return pl.pallas_call(
        functools.partial(weight_kernel, factor),
        grid=(depth // width,),
        out_shape=[jax.ShapeDtypeStruct((MAIN + TAIL, depth), BF16)] * 3,
        in_specs=[column, column] + [pl.BlockSpec(q.shape, lambda i: (0, 0)) for q in chunks],
        out_specs=[out] * 3,
        scratch_shapes=[pltpu.VMEM((PACKED, tokens), BF16)],
        compiler_params=pltpu.CompilerParams(vmem_limit_bytes=40 * 2**20),
        cost_estimate=pl.CostEstimate(
            flops=6 * tokens * depth * (MAIN + TAIL), bytes_accessed=6 * MAIN * depth, transcendentals=0
        ),
        name="weight_products",
    )(x, g, *chunks)


def x_along(x, z, y, c, w):
    return (x + w, z, y, c)


def x_against(x, z, y, c, w):
    return (x - w, z, y, c)


def gather(tokens, out_grad):
    block = jnp.stack([tokens, out_grad])
    pair = jnp.stack([block, swap_cores(block)])
    line_across = send(block, lambda x, z, y, c, w: (x, z, y + 2, c))
    line_prev = send(pair, lambda x, z, y, c, w: (x, z, y + w, c))
    other = swap_cores(jnp.concatenate([line_prev, line_across[None]]))
    own = jnp.stack([pair, line_prev, other[1::-1], jnp.stack([line_across, other[2]])])
    prev = send(own, lambda x, z, y, c, w: (x, z + w, y, c))
    lines, cores = range(4), range(2)
    yield (own,), [(0, (l, c)) for l in lines for c in cores]
    last = yield prev
    half = after(own[:, 0], prev)
    following = swap_cores(prev)
    half = send(half, lambda x, z, y, c, w: (x, z + 2, y, c))
    last = yield (
        (prev, following),
        [b for l in lines for b in [(0, (l, 0)), (0, (l, 1)), (1, (FLIP[l], 1)), (1, (FLIP[l], 0))]],
    )
    other_half = swap_cores(after(half, last))
    yield (half, other_half), [b for l in lines for b in [(0, (l,)), (1, (FLIP[l],))]]


def local(tokens, out_grad, gate_weight, up_weight, down_weight):
    depth = tokens.shape[1]
    factor = 1.0 / math.sqrt(tokens.shape[0] * PLANES * LINES * CORES)
    me = lax.axis_index("row")
    way = 1 - 2 * lax.rem(lax.axis_index("col"), CORES)
    at = jnp.stack([lax.rem(me + off + 4, 4) for off in (0, -way, way, 2)])
    weights = (gate_weight.T, up_weight.T, down_weight)
    ends = [jnp.pad(w[MAIN:], ((0, STEP - TAIL), (0, 0))) for w in weights]
    none = jnp.zeros_like(ends[0])
    tails = (
        jnp.concatenate([ends[0], ends[1], none, none]),
        jnp.concatenate([none, none, ends[2], none]),
        jnp.concatenate([none, ends[0], ends[1], none]),
    )

    chunks = gather(tokens, out_grad)
    last = None
    state = [{} for _ in range(3)]

    for i, s in enumerate(state):
        sources, layout = chunks.send(last)
        if last is not None:
            sources = after(sources, last)
        s["x"], s["g"], far, near, relay, own = forward(at, weights, tails, sources, layout)
        near = send(near, x_against)
        relay = (relay + send(far, x_along).astype(F32)).astype(BF16)
        if i == 0:
            prev = next(chunks)
            own = after(own, prev)
        mine = activation(own, near, send(relay, x_along))
        behind = send(mine, x_along)
        ahead = send(mine, x_against)
        pieces = (mine, behind, ahead, send(behind, x_along))
        q, keep, away = input_gradient(at, weights, tails[2], pieces)
        s["q"] = q.reshape(-1, PACKED)
        s["here"] = keep, swap_cores(away)
        if i == 0:
            last = mine
            first = (behind, ahead)
        else:
            last = first

    total = sum(state[0]["here"])
    here = sum(state[1]["here"])
    got = send(here.astype(BF16), lambda x, z, y, c, w: (x, z - w, y, c))
    here = sum(state[2]["here"])
    total += send(here.astype(BF16), lambda x, z, y, c, w: (x, z + 2, y, c)).astype(F32)
    all_x, all_g, all_q = ([s[k] for s in state] for k in ("x", "g", "q"))
    gate_wgrad, up_wgrad, down_wgrad = weight_gradients(
        after(jnp.concatenate(all_x), here), jnp.concatenate(all_g), all_q, factor
    )
    got = after(got, down_wgrad)
    rest = swap_cores(flip(got[:, 1]))
    total += got[:, 0].astype(F32) + rest.astype(F32)
    sent = total.astype(BF16)
    input_grad = (
        total[0]
        + send(sent[1], lambda x, z, y, c, w: (x, z, y - w, c)).astype(F32)
        + send(sent[2], lambda x, z, y, c, w: (x, z, y + w, c)).astype(F32)
        + send(sent[3], lambda x, z, y, c, w: (x, z, y + 2, c)).astype(F32)
    ).astype(BF16)
    return (input_grad, gate_wgrad.T, up_wgrad.T, down_wgrad)


def solution(mesh):
    placed = (P("col", "row"), P("col", "row"), P("row", "col"), P("row", "col"), P("col", "row"))
    return jax.shard_map(
        local,
        mesh=mesh,
        in_specs=placed,
        out_specs=(P("col", "row"), P("row", "col"), P("row", "col"), P("col", "row")),
        check_vma=False,
    )
```

time: 327 us -> 146 us (0.45)
  waiting for transfers between devices: 269 us -> 51.2 us
  starting transfers between devices: 0.34 us -> 49.4 us
  Pallas kernels: 0 us -> 37 us
  matrix products: 36.7 us -> 0 us
  between operations: 13.8 us -> 0.95 us
  local copies, waits for them, and re-layouts: 0.03 us -> 4.36 us
    psum x1 -> x0, waiting for transfers between devices: 116 us -> none  [local(): gate, upward, hid_grad = lax.psum((gate_part, up_part, grad_part), 'row')]
    all_gather x2 -> x0, waiting for transfers between devices: 85.1 us -> none  [the longest x1 49.2 us: local(): lax.all_gather(tokens, 'col', axis=0, tiled=True)]
    reduce_scatter x1 -> x0, waiting for transfers between devices: 66.6 us -> none  [local(): lax.psum_scatter(contract(gate_grad, gate_weight, 1, 1) + contract(up_gra...]
    ppermute x0 -> x35, waiting for transfers between devices: none -> 51.2 us  [send(): return lax.ppermute(value, ('row', 'col'), pairs)]
    ppermute x0 -> x35, starting transfers between devices: none -> 49.4 us  [send(): return lax.ppermute(value, ('row', 'col'), pairs)]
    pallas_call x0 -> x10, Pallas kernels: none -> 37 us  [the longest x3 18.8 us: forward(): call(kernel, [((rows, depth), BF16)] * 2 + [((count, PACKED), BF16)] * 2...]
    dot_general x8 -> x0, matrix products: 36.7 us -> none  [the longest x6 27 us: contract(): lax.dot_general(left, right, (((left_dim,), (right_dim,)), ((), ())), pre...]
    convert_element_type x2 -> x6, other arithmetic: 5.43 us -> 1.09 us  [the longest x1 0.66 us: local(): input_grad = (total[0] + send(sent[1], lambda x, z, y, c, w: (x, z, y - w...]
  transfers between devices with their start and end apart: 4 -> 35, of which waited for: 4 -> 19; matrix products, arithmetic and copies ran while one was open for 7% -> 2% of each run, Pallas kernels for 0% -> 25%
where the time goes in v1:
time: 146 us
  waiting for transfers between devices  51.2 us (35%)
  starting transfers between devices  49.4 us (34%)
  Pallas kernels  37 us (25%)
  local copies, waits for them, and re-layouts  4.36 us (3%)
  other arithmetic  3.09 us (2%)
    ppermute x35, waiting for transfers between devices, send(): return lax.ppermute(value, ('row', 'col'), pairs)  51.2 us
    ppermute x35, starting transfers between devices, send(): return lax.ppermute(value, ('row', 'col'), pairs)  49.4 us
    pallas_call x3, Pallas kernels, forward(): call(kernel, [((rows, depth), BF16)] * 2 + [((count, PACKED), BF16)] * 2...  18.8 us
    pallas_call x1, Pallas kernels, weight_gradients(): pl.pallas_call(functools.partial(weight_kernel, factor), grid=(depth // w...  10.3 us
    pallas_call x3, Pallas kernels, input_gradient(): call(functools.partial(input_kernel, planes), [((4, count, PACKED), BF16)...  7.17 us
  transfers between devices with their start and end apart: 35, of which 19 were waited for; matrix products, arithmetic and copies ran while one was open for 2% of the time, Pallas kernels for 25%

profile of v1, /device:TPU:1, one launch (start us, length us, event | category | flops | bytes accessed | tf_op | source)
XLA Modules:
  0.0 146.0 jit_solution(12814705185058550937)
XLA Ops:
  0.6 0.9 fusion.8
  1.6 1.5 %collective-permute-start = (bf16[2,16,2048]{2,1,0:T(8,128)(2,1)S(1)}, bf16[2,16,2048]{2,1,0:T(8,128)(2,1)S(1)}, u32[]{:S(2)}, u32[]{:S(2)}) collective-permute-start(bf16[2,16,2048]{2,1,0:T(8,128)(2,1)S(1)} %get-tuple-element.97), channel_id=1, source_target_pairs={{0,1},{1,0},{2,3},{3,2},{4,5},{5,4},{6,7},{7,6},{8,9},{9,8},{10,11... | collective-permute-start | bytes 393224 | tf_op jit(solution)/shard_map/ppermute | solution.py:34
  3.1 1.0 collective-permute-done
  4.1 2.9 %collective-permute-start.1 = (bf16[2,2,16,2048]{3,2,1,0:T(8,128)(2,1)S(1)}, bf16[2,2,16,2048]{3,2,1,0:T(8,128)(2,1)S(1)}, u32[]{:S(2)}, u32[]{:S(2)}) collective-permute-start(bf16[2,2,16,2048]{3,2,1,0:T(8,128)(2,1)S(1)} %get-tuple-element.92), channel_id=1, source_target_pairs={{0,2},{1,7},{2,4},{3,1},{4,6},{5,3},{6,0},{7,5},{8,10},{9,15},{10,... | collective-permute-start | bytes 786440 | tf_op jit(solution)/shard_map/ppermute | solution.py:34
  7.0 0.3 collective-permute-start.2
  7.3 6.4 %collective-permute-done.2 = bf16[2,16,2048]{2,1,0:T(8,128)(2,1)S(1)} collective-permute-done((bf16[2,16,2048]{2,1,0:T(8,128)(2,1)S(1)}, bf16[2,16,2048]{2,1,0:T(8,128)(2,1)S(1)}, u32[]{:S(2)}, u32[]{:S(2)}) %collective-permute-start.2) | collective-permute-done | bytes 131104 | tf_op jit(solution)/shard_map/ppermute | solution.py:34
  13.8 2.6 %collective-permute-start.3 = (bf16[3,2,16,2048]{3,2,1,0:T(8,128)(2,1)S(1)}, bf16[3,2,16,2048]{3,2,1,0:T(8,128)(2,1)S(1)}, u32[]{:S(2)}, u32[]{:S(2)}) collective-permute-start(bf16[3,2,16,2048]{3,2,1,0:T(8,128)(2,1)S(1)} %pad_maximum_fusion.6), channel_id=1, source_target_pairs={{0,1},{1,0},{2,3},{3,2},{4,5},{5,4},{6,7},{7,6},{8,9},{9,8},{10,11... | collective-permute-start | bytes 1179656 | tf_op jit(solution)/shard_map/ppermute | solution.py:34
  16.4 1.3 collective-permute-done.3
  17.9 3.8 %collective-permute-start.4 = (bf16[4,2,2,16,2048]{4,3,2,1,0:T(8,128)(2,1)S(1)}, bf16[4,2,2,16,2048]{4,3,2,1,0:T(8,128)(2,1)S(1)}, u32[]{:S(2)}, u32[]{:S(2)}) collective-permute-start(bf16[4,2,2,16,2048]{4,3,2,1,0:T(8,128)(2,1)S(1)} %pad_maximum_fusion.2.refs_0_), channel_id=1, source_target_pairs={{0,8},{1,25},{2,10},{3,27},{4,12},{5,29},{6,14},{7,31},{8,16},{9,1... | collective-permute-start | bytes 3145736 | tf_op jit(solution)/shard_map/ppermute | solution.py:34
  21.8 1.1 slice.81
  22.8 1.1 slice.82
  24.1 0.2 pad_maximum_fusion.3
  24.3 2.1 %copy-done.1 = bf16[2048,924]{0,1:T(8,128)(2,1)S(1)} copy-done((bf16[2048,924]{0,1:T(8,128)(2,1)S(1)}, bf16[2048,924]{0,1:T(8,128)(2,1)}, u32[]{:S(2)}) %copy-start.1) | copy-done | bytes 3784728
  26.3 5.6 %forward_products.3 = (bf16[128,2048]{1,0:T(8,128)(2,1)S(1)}, bf16[128,2048]{1,0:T(8,128)(2,1)S(1)}, bf16[32,2816]{1,0:T(8,128)(2,1)S(1)}, bf16[32,2816]{1,0:T(8...) custom-call(s32[4]{0:T(128)S(1)} %pad_add_fusion.at, bf16[924,2048]{1,0:T(8,128)(2,1)S(1)} %bitcast.57, ...), custom_call_target="tpu_custom_call" | custom-call | flops 1453326336 | bytes 11010048 | tf_op jit(solution)/shard_map/forward_products/pallas_call | solution.py:89
  31.9 2.5 %collective-permute-start.6 = (bf16[32,2816]{1,0:T(8,128)(2,1)S(1)}, bf16[32,2816]{1,0:T(8,128)(2,1)S(1)}, u32[]{:S(2)}, u32[]{:S(2)}) collective-permute-start(bf16[32,2816]{1,0:T(8,128)(2,1)S(1)} %get-tuple-element.47), channel_id=1, source_target_pairs={{0,32},{1,97},{2,34},{3,99},{4,36},{5,101},{6,38},{7,103},{8,40},{... | collective-permute-start | bytes 540680 | tf_op jit(solution)/shard_map/ppermute | solution.py:34
  34.5 0.7 collective-permute-start.22
  35.2 3.1 %collective-permute-done.6 = bf16[32,2816]{1,0:T(8,128)(2,1)S(1)} collective-permute-done((bf16[32,2816]{1,0:T(8,128)(2,1)S(1)}, bf16[32,2816]{1,0:T(8,128)(2,1)S(1)}, u32[]{:S(2)}, u32[]{:S(2)}) %collective-permute-start.6) | collective-permute-done | bytes 180256 | tf_op jit(solution)/shard_map/ppermute | solution.py:34
  38.3 3.2 %collective-permute-start.7 = (bf16[32,2816]{1,0:T(8,128)(2,1)S(1)}, bf16[32,2816]{1,0:T(8,128)(2,1)S(1)}, u32[]{:S(2)}, u32[]{:S(2)}) collective-permute-start(bf16[32,2816]{1,0:T(8,128)(2,1)S(1)} %add_convert_fusion.3), channel_id=1, source_target_pairs={{0,32},{1,97},{2,34},{3,99},{4,36},{5,101},{6,38},{7,103},{8,40},{... | collective-permute-start | bytes 540680 | tf_op jit(solution)/shard_map/ppermute | solution.py:34
  41.7 2.3 %collective-permute-done.7.relay = bf16[32,2816]{1,0:T(8,128)(2,1)S(1)} collective-permute-done((bf16[32,2816]{1,0:T(8,128)(2,1)S(1)}, bf16[32,2816]{1,0:T(8,128)(2,1)S(1)}, u32[]{:S(2)}, u32[]{:S(2)}) %collective-permute-start.7) | collective-permute-done | bytes 180256 | tf_op jit(solution)/shard_map/ppermute | solution.py:34
  44.0 0.2 activation.3.mine
  44.2 7.7 %forward_products.5 = (bf16[256,2048]{1,0:T(8,128)(2,1)S(1)}, bf16[256,2048]{1,0:T(8,128)(2,1)S(1)}, bf16[64,2816]{1,0:T(8,128)(2,1)S(1)}, bf16[64,2816]{1,0:T(8...) custom-call(s32[4]{0:T(128)S(1)} %pad_add_fusion.at, bf16[924,2048]{1,0:T(8,128)(2,1)S(1)} %bitcast.58, ...), custom_call_target="tpu_custom_call" | custom-call | flops 2906652672 | bytes 11010048 | tf_op jit(solution)/shard_map/forward_products/pallas_call | solution.py:89
  51.9 3.5 %collective-permute-start.24 = (bf16[64,2816]{1,0:T(8,128)(2,1)S(1)}, bf16[64,2816]{1,0:T(8,128)(2,1)S(1)}, u32[]{:S(2)}, u32[]{:S(2)}) collective-permute-start(bf16[64,2816]{1,0:T(8,128)(2,1)S(1)} %get-tuple-element.65), channel_id=1, source_target_pairs={{0,32},{1,97},{2,34},{3,99},{4,36},{5,101},{6,38},{7,103},{8,40},{... | collective-permute-start | bytes 1081352 | tf_op jit(solution)/shard_map/ppermute | solution.py:34
  55.3 2.7 %collective-permute-start.8 = (bf16[32,2816]{1,0:T(8,128)(2,1)S(1)}, bf16[32,2816]{1,0:T(8,128)(2,1)S(1)}, u32[]{:S(2)}, u32[]{:S(2)}) collective-permute-start(bf16[32,2816]{1,0:T(8,128)(2,1)S(1)} %activation.3.mine), channel_id=1, source_target_pairs={{0,32},{1,97},{2,34},{3,99},{4,36},{5,101},{6,38},{7,103},{8,40},{... | collective-permute-start | bytes 540680 | tf_op jit(solution)/shard_map/ppermute | solution.py:34
  58.0 5.2 %collective-permute-done.9.ahead = bf16[32,2816]{1,0:T(8,128)(2,1)S(1)} collective-permute-done((bf16[32,2816]{1,0:T(8,128)(2,1)S(1)}, bf16[32,2816]{1,0:T(8,128)(2,1)S(1)}, u32[]{:S(2)}, u32[]{:S(2)}) %collective-permute-start.9) | collective-permute-done | bytes 180256 | tf_op jit(solution)/shard_map/ppermute | solution.py:34
  63.2 0.4 collective-permute-done.8.behind
  63.6 0.9 collective-permute-start.13
  64.6 2.7 %collective-permute-start.25 = (bf16[64,2816]{1,0:T(8,128)(2,1)S(1)}, bf16[64,2816]{1,0:T(8,128)(2,1)S(1)}, u32[]{:S(2)}, u32[]{:S(2)}) collective-permute-start(bf16[64,2816]{1,0:T(8,128)(2,1)S(1)} %add_convert_fusion.1), channel_id=1, source_target_pairs={{0,32},{1,97},{2,34},{3,99},{4,36},{5,101},{6,38},{7,103},{8,40},{... | collective-permute-start | bytes 1081352 | tf_op jit(solution)/shard_map/ppermute | solution.py:34
  67.3 5.1 %collective-permute-done.23.near = bf16[64,2816]{1,0:T(8,128)(2,1)S(1)} collective-permute-done((bf16[64,2816]{1,0:T(8,128)(2,1)S(1)}, bf16[64,2816]{1,0:T(8,128)(2,1)S(1)}, u32[]{:S(2)}, u32[]{:S(2)}) %collective-permute-start.23) | collective-permute-done | bytes 360480 | tf_op jit(solution)/shard_map/ppermute | solution.py:34
  72.5 2.8 %collective-permute-done.25.relay = bf16[64,2816]{1,0:T(8,128)(2,1)S(1)} collective-permute-done((bf16[64,2816]{1,0:T(8,128)(2,1)S(1)}, bf16[64,2816]{1,0:T(8,128)(2,1)S(1)}, u32[]{:S(2)}, u32[]{:S(2)}) %collective-permute-start.25) | collective-permute-done | bytes 360480 | tf_op jit(solution)/shard_map/ppermute | solution.py:34
  75.2 0.3 activation.5.mine
  75.5 3.5 %collective-permute-start.26 = (bf16[64,2816]{1,0:T(8,128)(2,1)S(1)}, bf16[64,2816]{1,0:T(8,128)(2,1)S(1)}, u32[]{:S(2)}, u32[]{:S(2)}) collective-permute-start(bf16[64,2816]{1,0:T(8,128)(2,1)S(1)} %activation.5.mine), channel_id=1, source_target_pairs={{0,32},{1,97},{2,34},{3,99},{4,36},{5,101},{6,38},{7,103},{8,40},{... | collective-permute-start | bytes 1081352 | tf_op jit(solution)/shard_map/ppermute | solution.py:34
  79.0 5.6 %forward_products.4 = (bf16[128,2048]{1,0:T(8,128)(2,1)S(1)}, bf16[128,2048]{1,0:T(8,128)(2,1)S(1)}, bf16[32,2816]{1,0:T(8,128)(2,1)S(1)}, bf16[32,2816]{1,0:T(8...) custom-call(s32[4]{0:T(128)S(1)} %pad_add_fusion.at, bf16[924,2048]{1,0:T(8,128)(2,1)S(1)} %bitcast.59, ...), custom_call_target="tpu_custom_call" | custom-call | flops 1453326336 | bytes 11010048 | tf_op jit(solution)/shard_map/forward_products/pallas_call | solution.py:89
  84.7 1.4 collective-permute-start.14
  86.1 2.6 %collective-permute-start.28 = (bf16[64,2816]{1,0:T(8,128)(2,1)S(1)}, bf16[64,2816]{1,0:T(8,128)(2,1)S(1)}, u32[]{:S(2)}, u32[]{:S(2)}) collective-permute-start(bf16[64,2816]{1,0:T(8,128)(2,1)S(1)} %collective-permute-done.26.behind), channel_id=1, source_target_pairs={{0,32},{1,97},{2,34},{3,99},{4,36},{5,101},{6,38},{7,103},{8,40},{... | collective-permute-start | bytes 1081352 | tf_op jit(solution)/shard_map/ppermute | solution.py:34
  88.8 1.6 %collective-permute-done.15 = bf16[32,2816]{1,0:T(8,128)(2,1)S(1)} collective-permute-done((bf16[32,2816]{1,0:T(8,128)(2,1)S(1)}, bf16[32,2816]{1,0:T(8,128)(2,1)S(1)}, u32[]{:S(2)}, u32[]{:S(2)}) %collective-permute-start.15) | collective-permute-done | bytes 180256 | tf_op jit(solution)/shard_map/ppermute | solution.py:34
  90.4 0.7 collective-permute-start.16
  91.1 5.9 %collective-permute-done.27.ahead = bf16[64,2816]{1,0:T(8,128)(2,1)S(1)} collective-permute-done((bf16[64,2816]{1,0:T(8,128)(2,1)S(1)}, bf16[64,2816]{1,0:T(8,128)(2,1)S(1)}, u32[]{:S(2)}, u32[]{:S(2)}) %collective-permute-start.27) | collective-permute-done | bytes 360480 | tf_op jit(solution)/shard_map/ppermute | solution.py:34
  97.1 1.0 collective-permute-done.28.across
  98.1 3.2 %input_products.5 = (bf16[4,64,2816]{2,1,0:T(8,128)(2,1)S(1)}, f32[4,2,16,2048]{3,2,1,0:T(8,128)S(1)}, f32[4,2,16,2048]{3,2,1,0:T(8,128)S(1)}) custom-call(s32[4]{0:T(128)S(1)} %pad_add_fusion.at, bf16[924,2048]{1,0:T(8,128)(2,1)S(1)} %bitcast.60, bf16[924,2048]{1,0:T(8,128)(2,1)S(1)} %bitcast.67, bf16[128,2048]{1,0:T(8,128)(2,1)S(1)} %get-tuple-element.95.tail, ...), custom_call_target="tpu_custom_call" | custom-call | flops 1937768448 | bytes 7340032 | tf_op jit(solution)/shard_map/input_products/pallas_call | solution.py:171
  101.3 2.2 %collective-permute-start.29 = (f32[4,2,16,2048]{3,2,1,0:T(8,128)S(1)}, f32[4,2,16,2048]{3,2,1,0:T(8,128)S(1)}, u32[]{:S(2)}, u32[]{:S(2)}) collective-permute-start(f32[4,2,16,2048]{3,2,1,0:T(8,128)S(1)} %get-tuple-element.67), channel_id=1, source_target_pairs={{0,1},{1,0},{2,3},{3,2},{4,5},{5,4},{6,7},{7,6},{8,9},{9,8},{10,11... | collective-permute-start | bytes 3145736 | tf_op jit(solution)/shard_map/ppermute | solution.py:34
  103.5 0.2 activation.4.mine
  103.7 0.1 collective-permute-start.17
  103.8 1.1 collective-permute-start.10
  105.0 0.3 collective-permute-start.18
  105.3 3.1 %collective-permute-done.17.behind = bf16[32,2816]{1,0:T(8,128)(2,1)S(1)} collective-permute-done((bf16[32,2816]{1,0:T(8,128)(2,1)S(1)}, bf16[32,2816]{1,0:T(8,128)(2,1)S(1)}, u32[]{:S(2)}, u32[]{:S(2)}) %collective-permute-start.17) | collective-permute-done | bytes 180256 | tf_op jit(solution)/shard_map/ppermute | solution.py:34
  108.4 1.0 collective-permute-start.19
  109.4 2.6 %collective-permute-done.10.across = bf16[32,2816]{1,0:T(8,128)(2,1)S(1)} collective-permute-done((bf16[32,2816]{1,0:T(8,128)(2,1)S(1)}, bf16[32,2816]{1,0:T(8,128)(2,1)S(1)}, u32[]{:S(2)}, u32[]{:S(2)}) %collective-permute-start.10) | collective-permute-done | bytes 180256 | tf_op jit(solution)/shard_map/ppermute | solution.py:34
  111.9 2.0 %input_products.3 = (bf16[4,32,2816]{2,1,0:T(8,128)(2,1)S(1)}, f32[4,16,2048]{2,1,0:T(8,128)S(1)}, f32[4,16,2048]{2,1,0:T(8,128)S(1)}) custom-call(s32[4]{0:T(128)S(1)} %pad_add_fusion.at, bf16[924,2048]{1,0:T(8,128)(2,1)S(1)} %bitcast.61, bf16[924,2048]{1,0:T(8,128)(2,1)S(1)} %bitcast.68, bf16[128,2048]{1,0:T(8,128)(2,1)S(1)} %get-tuple-element.95.tail, ...), custom_call_target="tpu_custom_call" | custom-call | flops 968884224 | bytes 7340032 | tf_op jit(solution)/shard_map/input_products/pallas_call | solution.py:171
  113.9 2.7 %collective-permute-start.11 = (f32[4,16,2048]{2,1,0:T(8,128)S(1)}, f32[4,16,2048]{2,1,0:T(8,128)S(1)}, u32[]{:S(2)}, u32[]{:S(2)}) collective-permute-start(f32[4,16,2048]{2,1,0:T(8,128)S(1)} %get-tuple-element.49), channel_id=1, source_target_pairs={{0,1},{1,0},{2,3},{3,2},{4,5},{5,4},{6,7},{7,6},{8,9},{9,8},{10,11... | collective-permute-start | bytes 1572872 | tf_op jit(solution)/shard_map/ppermute | solution.py:34
  116.6 2.0 %input_products.4 = (bf16[4,32,2816]{2,1,0:T(8,128)(2,1)S(1)}, f32[4,16,2048]{2,1,0:T(8,128)S(1)}, f32[4,16,2048]{2,1,0:T(8,128)S(1)}) custom-call(s32[4]{0:T(128)S(1)} %pad_add_fusion.at, bf16[924,2048]{1,0:T(8,128)(2,1)S(1)} %bitcast.62, bf16[924,2048]{1,0:T(8,128)(2,1)S(1)} %bitcast.69, bf16[128,2048]{1,0:T(8,128)(2,1)S(1)} %get-tuple-element.95.tail, ...), custom_call_target="tpu_custom_call" | custom-call | flops 968884224 | bytes 7340032 | tf_op jit(solution)/shard_map/input_products/pallas_call | solution.py:171
  118.6 1.9 %collective-permute-start.20 = (f32[4,16,2048]{2,1,0:T(8,128)S(1)}, f32[4,16,2048]{2,1,0:T(8,128)S(1)}, u32[]{:S(2)}, u32[]{:S(2)}) collective-permute-start(f32[4,16,2048]{2,1,0:T(8,128)S(1)} %get-tuple-element.59), channel_id=1, source_target_pairs={{0,1},{1,0},{2,3},{3,2},{4,5},{5,4},{6,7},{7,6},{8,9},{9,8},{10,11... | collective-permute-start | bytes 1572872 | tf_op jit(solution)/shard_map/ppermute | solution.py:34
  120.5 0.2 pad_maximum_fusion.x
  120.7 0.2 pad_maximum_fusion.1.g
  121.0 1.0 collective-permute-done.20
  122.1 1.2 collective-permute-start.21
  123.5 10.3 %weight_products.1 = (bf16[924,2048]{1,0:T(8,128)(2,1)}, bf16[924,2048]{1,0:T(8,128)(2,1)}, bf16[924,2048]{1,0:T(8,128)(2,1)}) custom-call(bf16[512,2048]{1,0:T(8,128)(2,1)S(1)} %pad_maximum_fusion.x, bf16[512,2048]{1,0:T(8,128)(2,1)S(1)} %pad_maximum_fusion.1.g, bf16[128,2816]{1,0:T(8,128)(2,1)S(1)} %bitcast.71, bf16[256,2816]{1,0:T(8,128)(2,1)S(1)} %bitcast.70, ...), custom_call_target="tpu_custom_call" | custom-call | flops 5813305344 | bytes 11010048 | tf_op jit(solution)/shard_map/weight_products/pallas_call | solution.py:206
  133.8 3.5 %collective-permute-done.30 = bf16[4,2,16,2048]{3,2,1,0:T(8,128)(2,1)S(1)} collective-permute-done((bf16[4,2,16,2048]{3,2,1,0:T(8,128)(2,1)S(1)}, bf16[4,2,16,2048]{3,2,1,0:T(8,128)(2,1)S(1)}, u32[]{:S(2)}, u32[]{:S(2)}) %collective-permute-start.30) | collective-permute-done | bytes 524320 | tf_op jit(solution)/shard_map/ppermute | solution.py:34
  137.5 1.5 %collective-permute-done.31 = bf16[4,16,2048]{2,1,0:T(8,128)(2,1)S(1)} collective-permute-done((bf16[4,16,2048]{2,1,0:T(8,128)(2,1)S(1)}, bf16[4,16,2048]{2,1,0:T(8,128)(2,1)S(1)}, u32[]{:S(2)}, u32[]{:S(2)}) %collective-permute-start.31) | collective-permute-done | bytes 262176 | tf_op jit(solution)/shard_map/ppermute | solution.py:34
  139.0 0.1 fusion.10
  139.2 1.3 collective-permute-start.34
  140.5 1.4 collective-permute-start.33
  141.9 3.2 %collective-permute-done.32 = bf16[16,2048]{1,0:T(8,128)(2,1)S(1)} collective-permute-done((bf16[16,2048]{1,0:T(8,128)(2,1)S(1)}, bf16[16,2048]{1,0:T(8,128)(2,1)S(1)}, u32[]{:S(2)}, u32[]{:S(2)}) %collective-permute-start.32) | collective-permute-done | bytes 65568 | tf_op jit(solution)/shard_map/ppermute | solution.py:34
  145.1 0.2 collective-permute-done.33
  145.3 0.7 fusion.7
  (52 shorter events, 1.4 us)
Async XLA Ops:
  0.6 23.4 %slice-start = ((bf16[924,2048]{1,0:T(8,128)(2,1)}), bf16[28,2048]{1,0:T(8,128)(2,1)S(1)}, s32[]{:S(2)}) async-start(bf16[924,2048]{1,0:T(8,128)(2,1)} %down_w.5), calls=%async_computation | async-start | bytes 262144 | tf_op jit(solution)/shard_map/slice | solution.py:258
  1.6 2.5 %collective-permute-start = (bf16[2,16,2048]{2,1,0:T(8,128)(2,1)S(1)}, bf16[2,16,2048]{2,1,0:T(8,128)(2,1)S(1)}, u32[]{:S(2)}, u32[]{:S(2)}) collective-permute-start(bf16[2,16,2048]{2,1,0:T(8,128)(2,1)S(1)} %get-tuple-element.97), channel_id=1, source_target_pairs={{0,1},{1,0},{2,3},{3,2},{4,5},{5,4},{6,7},{7,6},{8,9},{9,8},{10,11... | collective-permute-start | bytes 393224 | tf_op jit(solution)/shard_map/ppermute | solution.py:34
  4.1 9.6 %collective-permute-start.1 = (bf16[2,2,16,2048]{3,2,1,0:T(8,128)(2,1)S(1)}, bf16[2,2,16,2048]{3,2,1,0:T(8,128)(2,1)S(1)}, u32[]{:S(2)}, u32[]{:S(2)}) collective-permute-start(bf16[2,2,16,2048]{3,2,1,0:T(8,128)(2,1)S(1)} %get-tuple-element.92), channel_id=1, source_target_pairs={{0,2},{1,7},{2,4},{3,1},{4,6},{5,3},{6,0},{7,5},{8,10},{9,15},{10,... | collective-permute-start | bytes 786440 | tf_op jit(solution)/shard_map/ppermute | solution.py:34
  7.0 6.7 %collective-permute-start.2 = (bf16[2,16,2048]{2,1,0:T(8,128)(2,1)S(1)}, bf16[2,16,2048]{2,1,0:T(8,128)(2,1)S(1)}, u32[]{:S(2)}, u32[]{:S(2)}) collective-permute-start(bf16[2,16,2048]{2,1,0:T(8,128)(2,1)S(1)} %get-tuple-element.97), channel_id=1, source_target_pairs={{0,4},{1,5},{2,6},{3,7},{4,0},{5,1},{6,2},{7,3},{8,12},{9,13},{10,... | collective-permute-start | bytes 393224 | tf_op jit(solution)/shard_map/ppermute | solution.py:34
  13.8 4.0 %collective-permute-start.3 = (bf16[3,2,16,2048]{3,2,1,0:T(8,128)(2,1)S(1)}, bf16[3,2,16,2048]{3,2,1,0:T(8,128)(2,1)S(1)}, u32[]{:S(2)}, u32[]{:S(2)}) collective-permute-start(bf16[3,2,16,2048]{3,2,1,0:T(8,128)(2,1)S(1)} %pad_maximum_fusion.6), channel_id=1, source_target_pairs={{0,1},{1,0},{2,3},{3,2},{4,5},{5,4},{6,7},{7,6},{8,9},{9,8},{10,11... | collective-permute-start | bytes 1179656 | tf_op jit(solution)/shard_map/ppermute | solution.py:34
  17.9 16.5 %collective-permute-start.4 = (bf16[4,2,2,16,2048]{4,3,2,1,0:T(8,128)(2,1)S(1)}, bf16[4,2,2,16,2048]{4,3,2,1,0:T(8,128)(2,1)S(1)}, u32[]{:S(2)}, u32[]{:S(2)}) collective-permute-start(bf16[4,2,2,16,2048]{4,3,2,1,0:T(8,128)(2,1)S(1)} %pad_maximum_fusion.2.refs_0_), channel_id=1, source_target_pairs={{0,8},{1,25},{2,10},{3,27},{4,12},{5,29},{6,14},{7,31},{8,16},{9,1... | collective-permute-start | bytes 3145736 | tf_op jit(solution)/shard_map/ppermute | solution.py:34
  21.8 2.5 %copy-start = (bf16[2048,924]{0,1:T(8,128)(2,1)S(1)}, bf16[2048,924]{0,1:T(8,128)(2,1)}, u32[]{:S(2)}) copy-start(bf16[2048,924]{0,1:T(8,128)(2,1)} %param.7) | copy-start | bytes 11354116
  24.3 2.1 %copy-start.1 = (bf16[2048,924]{0,1:T(8,128)(2,1)S(1)}, bf16[2048,924]{0,1:T(8,128)(2,1)}, u32[]{:S(2)}) copy-start(bf16[2048,924]{0,1:T(8,128)(2,1)} %param.8) | copy-start | bytes 11354116
  31.9 6.4 %collective-permute-start.6 = (bf16[32,2816]{1,0:T(8,128)(2,1)S(1)}, bf16[32,2816]{1,0:T(8,128)(2,1)S(1)}, u32[]{:S(2)}, u32[]{:S(2)}) collective-permute-start(bf16[32,2816]{1,0:T(8,128)(2,1)S(1)} %get-tuple-element.47), channel_id=1, source_target_pairs={{0,32},{1,97},{2,34},{3,99},{4,36},{5,101},{6,38},{7,103},{8,40},{... | collective-permute-start | bytes 540680 | tf_op jit(solution)/shard_map/ppermute | solution.py:34
  34.5 7.2 %collective-permute-start.5 = (bf16[32,2816]{1,0:T(8,128)(2,1)S(1)}, bf16[32,2816]{1,0:T(8,128)(2,1)S(1)}, u32[]{:S(2)}, u32[]{:S(2)}) collective-permute-start(bf16[32,2816]{1,0:T(8,128)(2,1)S(1)} %get-tuple-element.45), channel_id=1, source_target_pairs={{0,96},{1,33},{2,98},{3,35},{4,100},{5,37},{6,102},{7,39},{8,104},... | collective-permute-start | bytes 540680 | tf_op jit(solution)/shard_map/ppermute | solution.py:34
  34.5 9.7 %collective-permute-start.22 = (bf16[4,2,2,16,2048]{4,3,2,1,0:T(8,128)(2,1)S(1)}, bf16[4,2,2,16,2048]{4,3,2,1,0:T(8,128)(2,1)S(1)}, u32[]{:S(2)}, u32[]{:S(2)}) collective-permute-start(bf16[4,2,2,16,2048]{4,3,2,1,0:T(8,128)(2,1)S(1)} %collective-permute-done.4.refs_0_), channel_id=1, source_target_pairs={{0,1},{1,0},{2,3},{3,2},{4,5},{5,4},{6,7},{7,6},{8,9},{9,8},{10,11... | collective-permute-start | bytes 3145736 | tf_op jit(solution)/shard_map/ppermute | solution.py:34
  38.3 5.6 %collective-permute-start.7 = (bf16[32,2816]{1,0:T(8,128)(2,1)S(1)}, bf16[32,2816]{1,0:T(8,128)(2,1)S(1)}, u32[]{:S(2)}, u32[]{:S(2)}) collective-permute-start(bf16[32,2816]{1,0:T(8,128)(2,1)S(1)} %add_convert_fusion.3), channel_id=1, source_target_pairs={{0,32},{1,97},{2,34},{3,99},{4,36},{5,101},{6,38},{7,103},{8,40},{... | collective-permute-start | bytes 540680 | tf_op jit(solution)/shard_map/ppermute | solution.py:34
  41.6 22.0 %collective-permute-start.12 = (bf16[4,2,16,2048]{3,2,1,0:T(8,128)(2,1)S(1)}, bf16[4,2,16,2048]{3,2,1,0:T(8,128)(2,1)S(1)}, u32[]{:S(2)}, u32[]{:S(2)}) collective-permute-start(bf16[4,2,16,2048]{3,2,1,0:T(8,128)(2,1)S(1)} %slice_bitcast_fusion), channel_id=1, source_target_pairs={{0,16},{1,17},{2,18},{3,19},{4,20},{5,21},{6,22},{7,23},{8,24},{9,... | collective-permute-start | bytes 1572872 | tf_op jit(solution)/shard_map/ppermute | solution.py:34
  44.2 34.9 %copy-start.2 = (bf16[2048,924]{0,1:T(8,128)(2,1)S(1)}, bf16[2048,924]{0,1:T(8,128)(2,1)}, u32[]{:S(2)}) copy-start(bf16[2048,924]{0,1:T(8,128)(2,1)} %param.8) | copy-start | bytes 11354116
  51.9 12.6 %collective-permute-start.24 = (bf16[64,2816]{1,0:T(8,128)(2,1)S(1)}, bf16[64,2816]{1,0:T(8,128)(2,1)S(1)}, u32[]{:S(2)}, u32[]{:S(2)}) collective-permute-start(bf16[64,2816]{1,0:T(8,128)(2,1)S(1)} %get-tuple-element.65), channel_id=1, source_target_pairs={{0,32},{1,97},{2,34},{3,99},{4,36},{5,101},{6,38},{7,103},{8,40},{... | collective-permute-start | bytes 1081352 | tf_op jit(solution)/shard_map/ppermute | solution.py:34
  55.3 7.8 %collective-permute-start.9 = (bf16[32,2816]{1,0:T(8,128)(2,1)S(1)}, bf16[32,2816]{1,0:T(8,128)(2,1)S(1)}, u32[]{:S(2)}, u32[]{:S(2)}) collective-permute-start(bf16[32,2816]{1,0:T(8,128)(2,1)S(1)} %activation.3.mine), channel_id=1, source_target_pairs={{0,96},{1,33},{2,98},{3,35},{4,100},{5,37},{6,102},{7,39},{8,104},... | collective-permute-start | bytes 540680 | tf_op jit(solution)/shard_map/ppermute | solution.py:34
  55.3 8.2 %collective-permute-start.8 = (bf16[32,2816]{1,0:T(8,128)(2,1)S(1)}, bf16[32,2816]{1,0:T(8,128)(2,1)S(1)}, u32[]{:S(2)}, u32[]{:S(2)}) collective-permute-start(bf16[32,2816]{1,0:T(8,128)(2,1)S(1)} %activation.3.mine), channel_id=1, source_target_pairs={{0,32},{1,97},{2,34},{3,99},{4,36},{5,101},{6,38},{7,103},{8,40},{... | collective-permute-start | bytes 540680 | tf_op jit(solution)/shard_map/ppermute | solution.py:34
  63.6 15.4 %collective-permute-start.13 = (bf16[4,2,16,2048]{3,2,1,0:T(8,128)(2,1)S(1)}, bf16[4,2,16,2048]{3,2,1,0:T(8,128)(2,1)S(1)}, u32[]{:S(2)}, u32[]{:S(2)}) collective-permute-start(bf16[4,2,16,2048]{3,2,1,0:T(8,128)(2,1)S(1)} %collective-permute-done.12.refs_0_), channel_id=1, source_target_pairs={{0,1},{1,0},{2,3},{3,2},{4,5},{5,4},{6,7},{7,6},{8,9},{9,8},{10,11... | collective-permute-start | bytes 1572872 | tf_op jit(solution)/shard_map/ppermute | solution.py:34
  64.5 8.0 %collective-permute-start.23 = (bf16[64,2816]{1,0:T(8,128)(2,1)S(1)}, bf16[64,2816]{1,0:T(8,128)(2,1)S(1)}, u32[]{:S(2)}, u32[]{:S(2)}) collective-permute-start(bf16[64,2816]{1,0:T(8,128)(2,1)S(1)} %get-tuple-element.63), channel_id=1, source_target_pairs={{0,96},{1,33},{2,98},{3,35},{4,100},{5,37},{6,102},{7,39},{8,104},... | collective-permute-start | bytes 1081352 | tf_op jit(solution)/shard_map/ppermute | solution.py:34
  64.6 10.6 %collective-permute-start.25 = (bf16[64,2816]{1,0:T(8,128)(2,1)S(1)}, bf16[64,2816]{1,0:T(8,128)(2,1)S(1)}, u32[]{:S(2)}, u32[]{:S(2)}) collective-permute-start(bf16[64,2816]{1,0:T(8,128)(2,1)S(1)} %add_convert_fusion.1), channel_id=1, source_target_pairs={{0,32},{1,97},{2,34},{3,99},{4,36},{5,101},{6,38},{7,103},{8,40},{... | collective-permute-start | bytes 1081352 | tf_op jit(solution)/shard_map/ppermute | solution.py:34
  75.5 10.6 %collective-permute-start.26 = (bf16[64,2816]{1,0:T(8,128)(2,1)S(1)}, bf16[64,2816]{1,0:T(8,128)(2,1)S(1)}, u32[]{:S(2)}, u32[]{:S(2)}) collective-permute-start(bf16[64,2816]{1,0:T(8,128)(2,1)S(1)} %activation.5.mine), channel_id=1, source_target_pairs={{0,32},{1,97},{2,34},{3,99},{4,36},{5,101},{6,38},{7,103},{8,40},{... | collective-permute-start | bytes 1081352 | tf_op jit(solution)/shard_map/ppermute | solution.py:34
  84.6 5.8 %collective-permute-start.15 = (bf16[32,2816]{1,0:T(8,128)(2,1)S(1)}, bf16[32,2816]{1,0:T(8,128)(2,1)S(1)}, u32[]{:S(2)}, u32[]{:S(2)}) collective-permute-start(bf16[32,2816]{1,0:T(8,128)(2,1)S(1)} %get-tuple-element.57), channel_id=1, source_target_pairs={{0,32},{1,97},{2,34},{3,99},{4,36},{5,101},{6,38},{7,103},{8,40},{... | collective-permute-start | bytes 540680 | tf_op jit(solution)/shard_map/ppermute | solution.py:34
  84.7 18.8 %collective-permute-start.14 = (bf16[32,2816]{1,0:T(8,128)(2,1)S(1)}, bf16[32,2816]{1,0:T(8,128)(2,1)S(1)}, u32[]{:S(2)}, u32[]{:S(2)}) collective-permute-start(bf16[32,2816]{1,0:T(8,128)(2,1)S(1)} %get-tuple-element.55), channel_id=1, source_target_pairs={{0,96},{1,33},{2,98},{3,35},{4,100},{5,37},{6,102},{7,39},{8,104},... | collective-permute-start | bytes 540680 | tf_op jit(solution)/shard_map/ppermute | solution.py:34
  86.1 11.0 %collective-permute-start.27 = (bf16[64,2816]{1,0:T(8,128)(2,1)S(1)}, bf16[64,2816]{1,0:T(8,128)(2,1)S(1)}, u32[]{:S(2)}, u32[]{:S(2)}) collective-permute-start(bf16[64,2816]{1,0:T(8,128)(2,1)S(1)} %activation.5.mine), channel_id=1, source_target_pairs={{0,96},{1,33},{2,98},{3,35},{4,100},{5,37},{6,102},{7,39},{8,104},... | collective-permute-start | bytes 1081352 | tf_op jit(solution)/shard_map/ppermute | solution.py:34
  86.1 11.9 %collective-permute-start.28 = (bf16[64,2816]{1,0:T(8,128)(2,1)S(1)}, bf16[64,2816]{1,0:T(8,128)(2,1)S(1)}, u32[]{:S(2)}, u32[]{:S(2)}) collective-permute-start(bf16[64,2816]{1,0:T(8,128)(2,1)S(1)} %collective-permute-done.26.behind), channel_id=1, source_target_pairs={{0,32},{1,97},{2,34},{3,99},{4,36},{5,101},{6,38},{7,103},{8,40},{... | collective-permute-start | bytes 1081352 | tf_op jit(solution)/shard_map/ppermute | solution.py:34
  90.4 13.1 %collective-permute-start.16 = (bf16[32,2816]{1,0:T(8,128)(2,1)S(1)}, bf16[32,2816]{1,0:T(8,128)(2,1)S(1)}, u32[]{:S(2)}, u32[]{:S(2)}) collective-permute-start(bf16[32,2816]{1,0:T(8,128)(2,1)S(1)} %add_convert_fusion.2), channel_id=1, source_target_pairs={{0,32},{1,97},{2,34},{3,99},{4,36},{5,101},{6,38},{7,103},{8,40},{... | collective-permute-start | bytes 540680 | tf_op jit(solution)/shard_map/ppermute | solution.py:34
  101.3 21.9 %collective-permute-start.29 = (f32[4,2,16,2048]{3,2,1,0:T(8,128)S(1)}, f32[4,2,16,2048]{3,2,1,0:T(8,128)S(1)}, u32[]{:S(2)}, u32[]{:S(2)}) collective-permute-start(f32[4,2,16,2048]{3,2,1,0:T(8,128)S(1)} %get-tuple-element.67), channel_id=1, source_target_pairs={{0,1},{1,0},{2,3},{3,2},{4,5},{5,4},{6,7},{7,6},{8,9},{9,8},{10,11... | collective-permute-start | bytes 3145736 | tf_op jit(solution)/shard_map/ppermute | solution.py:34
  103.7 4.7 %collective-permute-start.17 = (bf16[32,2816]{1,0:T(8,128)(2,1)S(1)}, bf16[32,2816]{1,0:T(8,128)(2,1)S(1)}, u32[]{:S(2)}, u32[]{:S(2)}) collective-permute-start(bf16[32,2816]{1,0:T(8,128)(2,1)S(1)} %activation.4.mine), channel_id=1, source_target_pairs={{0,32},{1,97},{2,34},{3,99},{4,36},{5,101},{6,38},{7,103},{8,40},{... | collective-permute-start | bytes 540680 | tf_op jit(solution)/shard_map/ppermute | solution.py:34
  103.8 8.1 %collective-permute-start.10 = (bf16[32,2816]{1,0:T(8,128)(2,1)S(1)}, bf16[32,2816]{1,0:T(8,128)(2,1)S(1)}, u32[]{:S(2)}, u32[]{:S(2)}) collective-permute-start(bf16[32,2816]{1,0:T(8,128)(2,1)S(1)} %collective-permute-done.8.behind), channel_id=1, source_target_pairs={{0,32},{1,97},{2,34},{3,99},{4,36},{5,101},{6,38},{7,103},{8,40},{... | collective-permute-start | bytes 540680 | tf_op jit(solution)/shard_map/ppermute | solution.py:34
  105.0 11.7 %collective-permute-start.18 = (bf16[32,2816]{1,0:T(8,128)(2,1)S(1)}, bf16[32,2816]{1,0:T(8,128)(2,1)S(1)}, u32[]{:S(2)}, u32[]{:S(2)}) collective-permute-start(bf16[32,2816]{1,0:T(8,128)(2,1)S(1)} %activation.4.mine), channel_id=1, source_target_pairs={{0,96},{1,33},{2,98},{3,35},{4,100},{5,37},{6,102},{7,39},{8,104},... | collective-permute-start | bytes 540680 | tf_op jit(solution)/shard_map/ppermute | solution.py:34
  108.4 8.2 %collective-permute-start.19 = (bf16[32,2816]{1,0:T(8,128)(2,1)S(1)}, bf16[32,2816]{1,0:T(8,128)(2,1)S(1)}, u32[]{:S(2)}, u32[]{:S(2)}) collective-permute-start(bf16[32,2816]{1,0:T(8,128)(2,1)S(1)} %collective-permute-done.17.behind), channel_id=1, source_target_pairs={{0,32},{1,97},{2,34},{3,99},{4,36},{5,101},{6,38},{7,103},{8,40},{... | collective-permute-start | bytes 540680 | tf_op jit(solution)/shard_map/ppermute | solution.py:34
  113.9 23.5 %collective-permute-start.11 = (f32[4,16,2048]{2,1,0:T(8,128)S(1)}, f32[4,16,2048]{2,1,0:T(8,128)S(1)}, u32[]{:S(2)}, u32[]{:S(2)}) collective-permute-start(f32[4,16,2048]{2,1,0:T(8,128)S(1)} %get-tuple-element.49), channel_id=1, source_target_pairs={{0,1},{1,0},{2,3},{3,2},{4,5},{5,4},{6,7},{7,6},{8,9},{9,8},{10,11... | collective-permute-start | bytes 1572872 | tf_op jit(solution)/shard_map/ppermute | solution.py:34
  118.6 3.4 %collective-permute-start.20 = (f32[4,16,2048]{2,1,0:T(8,128)S(1)}, f32[4,16,2048]{2,1,0:T(8,128)S(1)}, u32[]{:S(2)}, u32[]{:S(2)}) collective-permute-start(f32[4,16,2048]{2,1,0:T(8,128)S(1)} %get-tuple-element.59), channel_id=1, source_target_pairs={{0,1},{1,0},{2,3},{3,2},{4,5},{5,4},{6,7},{7,6},{8,9},{9,8},{10,11... | collective-permute-start | bytes 1572872 | tf_op jit(solution)/shard_map/ppermute | solution.py:34
  122.1 15.4 %collective-permute-start.21 = (bf16[4,16,2048]{2,1,0:T(8,128)(2,1)S(1)}, bf16[4,16,2048]{2,1,0:T(8,128)(2,1)S(1)}, u32[]{:S(2)}, u32[]{:S(2)}) collective-permute-start(bf16[4,16,2048]{2,1,0:T(8,128)(2,1)S(1)} %add.72), channel_id=1, source_target_pairs={{0,16},{1,17},{2,18},{3,19},{4,20},{5,21},{6,22},{7,23},{8,24},{9,... | collective-permute-start | bytes 786440 | tf_op jit(solution)/shard_map/ppermute | solution.py:34
  123.4 13.9 %collective-permute-start.30 = (bf16[4,2,16,2048]{3,2,1,0:T(8,128)(2,1)S(1)}, bf16[4,2,16,2048]{3,2,1,0:T(8,128)(2,1)S(1)}, u32[]{:S(2)}, u32[]{:S(2)}) collective-permute-start(bf16[4,2,16,2048]{3,2,1,0:T(8,128)(2,1)S(1)} %add_convert_fusion), channel_id=1, source_target_pairs={{0,24},{1,9},{2,26},{3,11},{4,28},{5,13},{6,30},{7,15},{8,0},{9,17... | collective-permute-start | bytes 1572872 | tf_op jit(solution)/shard_map/ppermute | solution.py:34
  137.4 1.6 %collective-permute-start.31 = (bf16[4,16,2048]{2,1,0:T(8,128)(2,1)S(1)}, bf16[4,16,2048]{2,1,0:T(8,128)(2,1)S(1)}, u32[]{:S(2)}, u32[]{:S(2)}) collective-permute-start(bf16[4,16,2048]{2,1,0:T(8,128)(2,1)S(1)} %pad_maximum_fusion.8), channel_id=1, source_target_pairs={{0,1},{1,0},{2,3},{3,2},{4,5},{5,4},{6,7},{7,6},{8,9},{9,8},{10,11... | collective-permute-start | bytes 786440 | tf_op jit(solution)/shard_map/ppermute | solution.py:34
  139.2 6.0 %collective-permute-start.32 = (bf16[16,2048]{1,0:T(8,128)(2,1)S(1)}, bf16[16,2048]{1,0:T(8,128)(2,1)S(1)}, u32[]{:S(2)}, u32[]{:S(2)}) collective-permute-start(bf16[16,2048]{1,0:T(8,128)(2,1)S(1)} %get-tuple-element.88), channel_id=1, source_target_pairs={{0,6},{1,3},{2,0},{3,5},{4,2},{5,7},{6,4},{7,1},{8,14},{9,11},{10,... | collective-permute-start | bytes 196616 | tf_op jit(solution)/shard_map/ppermute | solution.py:34
  139.2 5.9 %collective-permute-start.34 = (bf16[16,2048]{1,0:T(8,128)(2,1)S(1)}, bf16[16,2048]{1,0:T(8,128)(2,1)S(1)}, u32[]{:S(2)}, u32[]{:S(2)}) collective-permute-start(bf16[16,2048]{1,0:T(8,128)(2,1)S(1)} %get-tuple-element.89), channel_id=1, source_target_pairs={{0,4},{1,5},{2,6},{3,7},{4,0},{5,1},{6,2},{7,3},{8,12},{9,13},{10,... | collective-permute-start | bytes 196616 | tf_op jit(solution)/shard_map/ppermute | solution.py:34
  140.5 4.8 %collective-permute-start.33 = (bf16[16,2048]{1,0:T(8,128)(2,1)S(1)}, bf16[16,2048]{1,0:T(8,128)(2,1)S(1)}, u32[]{:S(2)}, u32[]{:S(2)}) collective-permute-start(bf16[16,2048]{1,0:T(8,128)(2,1)S(1)} %get-tuple-element.90), channel_id=1, source_target_pairs={{0,2},{1,7},{2,4},{3,1},{4,6},{5,3},{6,0},{7,5},{8,10},{9,15},{10,... | collective-permute-start | bytes 196616 | tf_op jit(solution)/shard_map/ppermute | solution.py:34

commit v2 on v1

--- a/solution.py
+++ b/solution.py
@@ -14,7 +14,7 @@
 FLIP = (0, 2, 1, 3)
 MAIN, TAIL, STEP, LANES = 896, 28, 32, 128
 PACKED = 3 * MAIN + LANES
-TILES = ((0, 256), (256, 256), (512, 256), (768, 128))
+TILES = ((0, MAIN),)
 VMEM = pl.BlockSpec(memory_space=pltpu.VMEM)
 SMEM = pl.BlockSpec(memory_space=pltpu.SMEM)
 
@@ -200,7 +200,7 @@
 
 def weight_gradients(x, g, chunks, factor):
     tokens, depth = x.shape
-    width = 256
+    width = 512
     column = pl.BlockSpec((tokens, width), lambda i: (0, i))
     out = pl.BlockSpec((MAIN + TAIL, width), lambda i: (0, i))
     return pl.pallas_call(
@@ -286,9 +286,8 @@
         s["here"] = keep, swap_cores(away)
         if i == 0:
             last = mine
-            first = (behind, ahead)
         else:
-            last = first
+            last = far
 
     total = sum(state[0]["here"])
     here = sum(state[1]["here"])

time: 146 us -> 143 us (0.979)
  waiting for transfers between devices: 51.2 us -> 42.1 us
  starting transfers between devices: 49.4 us -> 56.5 us
    ppermute x35, waiting for transfers between devices: 51.2 us -> 42.1 us  [send(): return lax.ppermute(value, ('row', 'col'), pairs)]
    ppermute x35, starting transfers between devices: 49.4 us -> 56.5 us  [send(): return lax.ppermute(value, ('row', 'col'), pairs)]
  transfers between devices with their start and end apart: 35 -> 35, of which waited for: 19 -> 17; matrix products, arithmetic and copies ran while one was open for 2% -> 2% of each run, Pallas kernels for 25% -> 25%
where the time goes in v2:
time: 143 us
  starting transfers between devices  56.5 us (40%)
  waiting for transfers between devices  42.1 us (29%)
  Pallas kernels  35.6 us (25%)
  local copies, waits for them, and re-layouts  4.6 us (3%)
  other arithmetic  3.06 us (2%)
    ppermute x35, starting transfers between devices, send(): return lax.ppermute(value, ('row', 'col'), pairs)  56.5 us
    ppermute x35, waiting for transfers between devices, send(): return lax.ppermute(value, ('row', 'col'), pairs)  42.1 us
    pallas_call x3, Pallas kernels, forward(): call(kernel, [((rows, depth), BF16)] * 2 + [((count, PACKED), BF16)] * 2...  18.4 us
    pallas_call x1, Pallas kernels, weight_gradients(): pl.pallas_call(functools.partial(weight_kernel, factor), grid=(depth // w...  9.42 us
    pallas_call x3, Pallas kernels, input_gradient(): call(functools.partial(input_kernel, planes), [((4, count, PACKED), BF16)...  7.18 us
  transfers between devices with their start and end apart: 35, of which 17 were waited for; matrix products, arithmetic and copies ran while one was open for 2% of the time, Pallas kernels for 25%

profile of v2, /device:TPU:1, one launch (start us, length us, event | category | flops | bytes accessed | tf_op | source)
XLA Modules:
  0.0 142.9 jit_solution(4052825266537544392)
XLA Ops:
  0.6 0.9 fusion.8
  1.6 1.5 %collective-permute-start = (bf16[2,16,2048]{2,1,0:T(8,128)(2,1)S(1)}, bf16[2,16,2048]{2,1,0:T(8,128)(2,1)S(1)}, u32[]{:S(2)}, u32[]{:S(2)}) collective-permute-start(bf16[2,16,2048]{2,1,0:T(8,128)(2,1)S(1)} %get-tuple-element.97), channel_id=1, source_target_pairs={{0,1},{1,0},{2,3},{3,2},{4,5},{5,4},{6,7},{7,6},{8,9},{9,8},{10,11... | collective-permute-start | bytes 393224 | tf_op jit(solution)/shard_map/ppermute | solution.py:34
  3.1 1.0 collective-permute-done
  4.1 2.9 %collective-permute-start.1 = (bf16[2,2,16,2048]{3,2,1,0:T(8,128)(2,1)S(1)}, bf16[2,2,16,2048]{3,2,1,0:T(8,128)(2,1)S(1)}, u32[]{:S(2)}, u32[]{:S(2)}) collective-permute-start(bf16[2,2,16,2048]{3,2,1,0:T(8,128)(2,1)S(1)} %get-tuple-element.92), channel_id=1, source_target_pairs={{0,2},{1,7},{2,4},{3,1},{4,6},{5,3},{6,0},{7,5},{8,10},{9,15},{10,... | collective-permute-start | bytes 786440 | tf_op jit(solution)/shard_map/ppermute | solution.py:34
  7.0 0.3 collective-permute-start.2
  7.3 6.4 %collective-permute-done.2 = bf16[2,16,2048]{2,1,0:T(8,128)(2,1)S(1)} collective-permute-done((bf16[2,16,2048]{2,1,0:T(8,128)(2,1)S(1)}, bf16[2,16,2048]{2,1,0:T(8,128)(2,1)S(1)}, u32[]{:S(2)}, u32[]{:S(2)}) %collective-permute-start.2) | collective-permute-done | bytes 131104 | tf_op jit(solution)/shard_map/ppermute | solution.py:34
  13.8 2.6 %collective-permute-start.3 = (bf16[3,2,16,2048]{3,2,1,0:T(8,128)(2,1)S(1)}, bf16[3,2,16,2048]{3,2,1,0:T(8,128)(2,1)S(1)}, u32[]{:S(2)}, u32[]{:S(2)}) collective-permute-start(bf16[3,2,16,2048]{3,2,1,0:T(8,128)(2,1)S(1)} %pad_maximum_fusion.6), channel_id=1, source_target_pairs={{0,1},{1,0},{2,3},{3,2},{4,5},{5,4},{6,7},{7,6},{8,9},{9,8},{10,11... | collective-permute-start | bytes 1179656 | tf_op jit(solution)/shard_map/ppermute | solution.py:34
  16.4 1.3 collective-permute-done.3
  17.8 0.1 pad_maximum_fusion.2
  17.9 3.8 %collective-permute-start.4 = (bf16[4,2,2,16,2048]{4,3,2,0,1:T(8,128)(2,1)S(1)}, bf16[4,2,2,16,2048]{4,3,2,0,1:T(8,128)(2,1)S(1)}, u32[]{:S(2)}, u32[]{:S(2)}) collective-permute-start(bf16[4,2,2,16,2048]{4,3,2,0,1:T(8,128)(2,1)S(1)} %pad_maximum_fusion.2), channel_id=1, source_target_pairs={{0,8},{1,25},{2,10},{3,27},{4,12},{5,29},{6,14},{7,31},{8,16},{9,1... | collective-permute-start | bytes 3145736 | tf_op jit(solution)/shard_map/ppermute | solution.py:34
  21.8 1.1 slice.81
  22.8 1.1 slice.82
  24.1 0.2 pad_maximum_fusion.3
  24.4 2.1 %copy-done.1 = bf16[2048,924]{0,1:T(8,128)(2,1)S(1)} copy-done((bf16[2048,924]{0,1:T(8,128)(2,1)S(1)}, bf16[2048,924]{0,1:T(8,128)(2,1)}, u32[]{:S(2)}) %copy-start.1) | copy-done | bytes 3784728
  26.4 5.6 %forward_products.3 = (bf16[128,2048]{1,0:T(8,128)(2,1)S(1)}, bf16[128,2048]{1,0:T(8,128)(2,1)S(1)}, bf16[32,2816]{1,0:T(8,128)(2,1)S(1)}, bf16[32,2816]{1,0:T(8...) custom-call(s32[4]{0:T(128)S(1)} %pad_add_fusion.at, bf16[924,2048]{1,0:T(8,128)(2,1)S(1)} %bitcast.63, ...), custom_call_target="tpu_custom_call" | custom-call | flops 1453326336 | bytes 11010048 | tf_op jit(solution)/shard_map/forward_products/pallas_call | solution.py:89
  32.0 2.5 %collective-permute-start.6 = (bf16[32,2816]{1,0:T(8,128)(2,1)S(1)}, bf16[32,2816]{1,0:T(8,128)(2,1)S(1)}, u32[]{:S(2)}, u32[]{:S(2)}) collective-permute-start(bf16[32,2816]{1,0:T(8,128)(2,1)S(1)} %get-tuple-element.47), channel_id=1, source_target_pairs={{0,32},{1,97},{2,34},{3,99},{4,36},{5,101},{6,38},{7,103},{8,40},{... | collective-permute-start | bytes 540680 | tf_op jit(solution)/shard_map/ppermute | solution.py:34
  34.5 0.7 collective-permute-start.13
  35.2 3.2 %collective-permute-done.6 = bf16[32,2816]{1,0:T(8,128)(2,1)S(1)} collective-permute-done((bf16[32,2816]{1,0:T(8,128)(2,1)S(1)}, bf16[32,2816]{1,0:T(8,128)(2,1)S(1)}, u32[]{:S(2)}, u32[]{:S(2)}) %collective-permute-start.6) | collective-permute-done | bytes 180256 | tf_op jit(solution)/shard_map/ppermute | solution.py:34
  38.4 3.2 %collective-permute-start.7 = (bf16[32,2816]{1,0:T(8,128)(2,1)S(1)}, bf16[32,2816]{1,0:T(8,128)(2,1)S(1)}, u32[]{:S(2)}, u32[]{:S(2)}) collective-permute-start(bf16[32,2816]{1,0:T(8,128)(2,1)S(1)} %add_convert_fusion.3), channel_id=1, source_target_pairs={{0,32},{1,97},{2,34},{3,99},{4,36},{5,101},{6,38},{7,103},{8,40},{... | collective-permute-start | bytes 540680 | tf_op jit(solution)/shard_map/ppermute | solution.py:34
  41.7 2.3 %collective-permute-done.7.relay = bf16[32,2816]{1,0:T(8,128)(2,1)S(1)} collective-permute-done((bf16[32,2816]{1,0:T(8,128)(2,1)S(1)}, bf16[32,2816]{1,0:T(8,128)(2,1)S(1)}, u32[]{:S(2)}, u32[]{:S(2)}) %collective-permute-start.7) | collective-permute-done | bytes 180256 | tf_op jit(solution)/shard_map/ppermute | solution.py:34
  44.0 0.2 activation.3.mine
  44.4 7.3 %forward_products.4 = (bf16[256,2048]{1,0:T(8,128)(2,1)S(1)}, bf16[256,2048]{1,0:T(8,128)(2,1)S(1)}, bf16[64,2816]{1,0:T(8,128)(2,1)S(1)}, bf16[64,2816]{1,0:T(8...) custom-call(s32[4]{0:T(128)S(1)} %pad_add_fusion.at, bf16[924,2048]{1,0:T(8,128)(2,1)S(1)} %bitcast.64, ...), custom_call_target="tpu_custom_call" | custom-call | flops 2906652672 | bytes 11010048 | tf_op jit(solution)/shard_map/forward_products/pallas_call | solution.py:89
  51.7 3.5 %collective-permute-start.24 = (bf16[64,2816]{1,0:T(8,128)(2,1)S(1)}, bf16[64,2816]{1,0:T(8,128)(2,1)S(1)}, u32[]{:S(2)}, u32[]{:S(2)}) collective-permute-start(bf16[64,2816]{1,0:T(8,128)(2,1)S(1)} %get-tuple-element.53), channel_id=1, source_target_pairs={{0,32},{1,97},{2,34},{3,99},{4,36},{5,101},{6,38},{7,103},{8,40},{... | collective-permute-start | bytes 1081352 | tf_op jit(solution)/shard_map/ppermute | solution.py:34
  55.2 0.3 collective-permute-start.23
  55.5 2.4 %collective-permute-start.14 = (bf16[4,2,16,2048]{3,2,1,0:T(8,128)(2,1)S(1)}, bf16[4,2,16,2048]{3,2,1,0:T(8,128)(2,1)S(1)}, u32[]{:S(2)}, u32[]{:S(2)}) collective-permute-start(bf16[4,2,16,2048]{3,2,1,0:T(8,128)(2,1)S(1)} %collective-permute-done.12.refs_0_), channel_id=1, source_target_pairs={{0,1},{1,0},{2,3},{3,2},{4,5},{5,4},{6,7},{7,6},{8,9},{9,8},{10,11... | collective-permute-start | bytes 1572872 | tf_op jit(solution)/shard_map/ppermute | solution.py:34
  57.9 2.6 %collective-permute-done.24 = bf16[64,2816]{1,0:T(8,128)(2,1)S(1)} collective-permute-done((bf16[64,2816]{1,0:T(8,128)(2,1)S(1)}, bf16[64,2816]{1,0:T(8,128)(2,1)S(1)}, u32[]{:S(2)}, u32[]{:S(2)}) %collective-permute-start.24) | collective-permute-done | bytes 360480 | tf_op jit(solution)/shard_map/ppermute | solution.py:34
  60.5 3.5 %collective-permute-start.25 = (bf16[64,2816]{1,0:T(8,128)(2,1)S(1)}, bf16[64,2816]{1,0:T(8,128)(2,1)S(1)}, u32[]{:S(2)}, u32[]{:S(2)}) collective-permute-start(bf16[64,2816]{1,0:T(8,128)(2,1)S(1)} %add_convert_fusion.1), channel_id=1, source_target_pairs={{0,32},{1,97},{2,34},{3,99},{4,36},{5,101},{6,38},{7,103},{8,40},{... | collective-permute-start | bytes 1081352 | tf_op jit(solution)/shard_map/ppermute | solution.py:34
  64.0 4.4 %collective-permute-done.25.relay = bf16[64,2816]{1,0:T(8,128)(2,1)S(1)} collective-permute-done((bf16[64,2816]{1,0:T(8,128)(2,1)S(1)}, bf16[64,2816]{1,0:T(8,128)(2,1)S(1)}, u32[]{:S(2)}, u32[]{:S(2)}) %collective-permute-start.25) | collective-permute-done | bytes 360480 | tf_op jit(solution)/shard_map/ppermute | solution.py:34
  68.4 0.3 activation.5.mine
  68.7 3.4 %collective-permute-start.26 = (bf16[64,2816]{1,0:T(8,128)(2,1)S(1)}, bf16[64,2816]{1,0:T(8,128)(2,1)S(1)}, u32[]{:S(2)}, u32[]{:S(2)}) collective-permute-start(bf16[64,2816]{1,0:T(8,128)(2,1)S(1)} %activation.5.mine), channel_id=1, source_target_pairs={{0,32},{1,97},{2,34},{3,99},{4,36},{5,101},{6,38},{7,103},{8,40},{... | collective-permute-start | bytes 1081352 | tf_op jit(solution)/shard_map/ppermute | solution.py:34
  72.0 5.6 %forward_products.5 = (bf16[128,2048]{1,0:T(8,128)(2,1)S(1)}, bf16[128,2048]{1,0:T(8,128)(2,1)S(1)}, bf16[32,2816]{1,0:T(8,128)(2,1)S(1)}, bf16[32,2816]{1,0:T(8...) custom-call(s32[4]{0:T(128)S(1)} %pad_add_fusion.at, bf16[924,2048]{1,0:T(8,128)(2,1)S(1)} %bitcast.65, ...), custom_call_target="tpu_custom_call" | custom-call | flops 1453326336 | bytes 11010048 | tf_op jit(solution)/shard_map/forward_products/pallas_call | solution.py:89
  77.8 1.4 %collective-permute-start.15 = (bf16[32,2816]{1,0:T(8,128)(2,1)S(1)}, bf16[32,2816]{1,0:T(8,128)(2,1)S(1)}, u32[]{:S(2)}, u32[]{:S(2)}) collective-permute-start(bf16[32,2816]{1,0:T(8,128)(2,1)S(1)} %get-tuple-element.58), channel_id=1, source_target_pairs={{0,96},{1,33},{2,98},{3,35},{4,100},{5,37},{6,102},{7,39},{8,104},... | collective-permute-start | bytes 540680 | tf_op jit(solution)/shard_map/ppermute | solution.py:34
  79.2 1.4 collective-permute-start.27
  80.6 1.3 collective-permute-start.28
  81.9 0.5 collective-permute-done.16
  82.5 0.9 collective-permute-start.17
  83.4 10.0 %collective-permute-done.27.ahead = bf16[64,2816]{1,0:T(8,128)(2,1)S(1)} collective-permute-done((bf16[64,2816]{1,0:T(8,128)(2,1)S(1)}, bf16[64,2816]{1,0:T(8,128)(2,1)S(1)}, u32[]{:S(2)}, u32[]{:S(2)}) %collective-permute-start.27) | collective-permute-done | bytes 360480 | tf_op jit(solution)/shard_map/ppermute | solution.py:34
  93.4 0.6 collective-permute-done.28.across
  93.9 3.2 %input_products.5 = (bf16[4,64,2816]{2,1,0:T(8,128)(2,1)S(1)}, f32[4,2,16,2048]{3,2,1,0:T(8,128)S(1)}, f32[4,2,16,2048]{3,2,1,0:T(8,128)S(1)}) custom-call(s32[4]{0:T(128)S(1)} %pad_add_fusion.at, bf16[924,2048]{1,0:T(8,128)(2,1)S(1)} %bitcast.66, bf16[924,2048]{1,0:T(8,128)(2,1)S(1)} %bitcast.73, bf16[128,2048]{1,0:T(8,128)(2,1)S(1)} %get-tuple-element.95.tail, ...), custom_call_target="tpu_custom_call" | custom-call | flops 1937768448 | bytes 7340032 | tf_op jit(solution)/shard_map/input_products/pallas_call | solution.py:171
  97.1 0.8 collective-permute-start.29
  98.0 0.2 activation.4.mine
  98.2 1.8 %collective-permute-start.18 = (bf16[32,2816]{1,0:T(8,128)(2,1)S(1)}, bf16[32,2816]{1,0:T(8,128)(2,1)S(1)}, u32[]{:S(2)}, u32[]{:S(2)}) collective-permute-start(bf16[32,2816]{1,0:T(8,128)(2,1)S(1)} %activation.4.mine), channel_id=1, source_target_pairs={{0,32},{1,97},{2,34},{3,99},{4,36},{5,101},{6,38},{7,103},{8,40},{... | collective-permute-start | bytes 540680 | tf_op jit(solution)/shard_map/ppermute | solution.py:34
  100.0 2.7 %collective-permute-start.10 = (bf16[32,2816]{1,0:T(8,128)(2,1)S(1)}, bf16[32,2816]{1,0:T(8,128)(2,1)S(1)}, u32[]{:S(2)}, u32[]{:S(2)}) collective-permute-start(bf16[32,2816]{1,0:T(8,128)(2,1)S(1)} %collective-permute-done.8.behind), channel_id=1, source_target_pairs={{0,32},{1,97},{2,34},{3,99},{4,36},{5,101},{6,38},{7,103},{8,40},{... | collective-permute-start | bytes 540680 | tf_op jit(solution)/shard_map/ppermute | solution.py:34
  102.6 0.2 collective-permute-done.18.behind
  102.9 3.1 %collective-permute-start.20 = (bf16[32,2816]{1,0:T(8,128)(2,1)S(1)}, bf16[32,2816]{1,0:T(8,128)(2,1)S(1)}, u32[]{:S(2)}, u32[]{:S(2)}) collective-permute-start(bf16[32,2816]{1,0:T(8,128)(2,1)S(1)} %collective-permute-done.18.behind), channel_id=1, source_target_pairs={{0,32},{1,97},{2,34},{3,99},{4,36},{5,101},{6,38},{7,103},{8,40},{... | collective-permute-start | bytes 540680 | tf_op jit(solution)/shard_map/ppermute | solution.py:34
  105.9 1.1 collective-permute-done.9.ahead
  107.1 2.0 %input_products.3 = (bf16[4,32,2816]{2,1,0:T(8,128)(2,1)S(1)}, f32[4,16,2048]{2,1,0:T(8,128)S(1)}, f32[4,16,2048]{2,1,0:T(8,128)S(1)}) custom-call(s32[4]{0:T(128)S(1)} %pad_add_fusion.at, bf16[924,2048]{1,0:T(8,128)(2,1)S(1)} %bitcast.67, bf16[924,2048]{1,0:T(8,128)(2,1)S(1)} %bitcast.74, bf16[128,2048]{1,0:T(8,128)(2,1)S(1)} %get-tuple-element.95.tail, ...), custom_call_target="tpu_custom_call" | custom-call | flops 968884224 | bytes 7340032 | tf_op jit(solution)/shard_map/input_products/pallas_call | solution.py:171
  109.1 3.2 %collective-permute-start.11 = (f32[4,16,2048]{2,1,0:T(8,128)S(1)}, f32[4,16,2048]{2,1,0:T(8,128)S(1)}, u32[]{:S(2)}, u32[]{:S(2)}) collective-permute-start(f32[4,16,2048]{2,1,0:T(8,128)S(1)} %get-tuple-element.49), channel_id=1, source_target_pairs={{0,1},{1,0},{2,3},{3,2},{4,5},{5,4},{6,7},{7,6},{8,9},{9,8},{10,11... | collective-permute-start | bytes 1572872 | tf_op jit(solution)/shard_map/ppermute | solution.py:34
  112.3 2.0 %input_products.4 = (bf16[4,32,2816]{2,1,0:T(8,128)(2,1)S(1)}, f32[4,16,2048]{2,1,0:T(8,128)S(1)}, f32[4,16,2048]{2,1,0:T(8,128)S(1)}) custom-call(s32[4]{0:T(128)S(1)} %pad_add_fusion.at, bf16[924,2048]{1,0:T(8,128)(2,1)S(1)} %bitcast.68, bf16[924,2048]{1,0:T(8,128)(2,1)S(1)} %bitcast.75, bf16[128,2048]{1,0:T(8,128)(2,1)S(1)} %get-tuple-element.95.tail, ...), custom_call_target="tpu_custom_call" | custom-call | flops 968884224 | bytes 7340032 | tf_op jit(solution)/shard_map/input_products/pallas_call | solution.py:171
  114.3 0.5 collective-permute-start.21
  114.8 0.2 pad_maximum_fusion.x
  115.0 0.2 pad_maximum_fusion.1.g
  115.2 1.0 collective-permute-done.21
  116.3 5.6 %collective-permute-start.22 = (bf16[4,16,2048]{2,1,0:T(8,128)(2,1)S(1)}, bf16[4,16,2048]{2,1,0:T(8,128)(2,1)S(1)}, u32[]{:S(2)}, u32[]{:S(2)}) collective-permute-start(bf16[4,16,2048]{2,1,0:T(8,128)(2,1)S(1)} %add.72), channel_id=1, source_target_pairs={{0,16},{1,17},{2,18},{3,19},{4,20},{5,21},{6,22},{7,23},{8,24},{9,... | collective-permute-start | bytes 786440 | tf_op jit(solution)/shard_map/ppermute | solution.py:34
  122.0 0.1 add_convert_fusion
  122.2 9.4 %weight_products.1 = (bf16[924,2048]{1,0:T(8,128)(2,1)}, bf16[924,2048]{1,0:T(8,128)(2,1)}, bf16[924,2048]{1,0:T(8,128)(2,1)}) custom-call(bf16[512,2048]{1,0:T(8,128)(2,1)S(1)} %pad_maximum_fusion.x, bf16[512,2048]{1,0:T(8,128)(2,1)S(1)} %pad_maximum_fusion.1.g, bf16[128,2816]{1,0:T(8,128)(2,1)S(1)} %bitcast.77, bf16[256,2816]{1,0:T(8,128)(2,1)S(1)} %bitcast.76, ...), custom_call_target="tpu_custom_call" | custom-call | flops 5813305344 | bytes 11010048 | tf_op jit(solution)/shard_map/weight_products/pallas_call | solution.py:206
  131.6 2.5 %collective-permute-done.30 = bf16[4,2,16,2048]{3,2,1,0:T(8,128)(2,1)S(1)} collective-permute-done((bf16[4,2,16,2048]{3,2,1,0:T(8,128)(2,1)S(1)}, bf16[4,2,16,2048]{3,2,1,0:T(8,128)(2,1)S(1)}, u32[]{:S(2)}, u32[]{:S(2)}) %collective-permute-start.30) | collective-permute-done | bytes 524320 | tf_op jit(solution)/shard_map/ppermute | solution.py:34
  134.3 1.5 %collective-permute-done.31 = bf16[4,16,2048]{2,1,0:T(8,128)(2,1)S(1)} collective-permute-done((bf16[4,16,2048]{2,1,0:T(8,128)(2,1)S(1)}, bf16[4,16,2048]{2,1,0:T(8,128)(2,1)S(1)}, u32[]{:S(2)}, u32[]{:S(2)}) %collective-permute-start.31) | collective-permute-done | bytes 262176 | tf_op jit(solution)/shard_map/ppermute | solution.py:34
  135.8 0.1 fusion.10
  136.1 1.6 %collective-permute-start.34 = (bf16[16,2048]{1,0:T(8,128)(2,1)S(1)}, bf16[16,2048]{1,0:T(8,128)(2,1)S(1)}, u32[]{:S(2)}, u32[]{:S(2)}) collective-permute-start(bf16[16,2048]{1,0:T(8,128)(2,1)S(1)} %get-tuple-element.89), channel_id=1, source_target_pairs={{0,4},{1,5},{2,6},{3,7},{4,0},{5,1},{6,2},{7,3},{8,12},{9,13},{10,... | collective-permute-start | bytes 196616 | tf_op jit(solution)/shard_map/ppermute | solution.py:34
  137.6 1.1 collective-permute-start.33
  138.8 2.3 %collective-permute-done.32 = bf16[16,2048]{1,0:T(8,128)(2,1)S(1)} collective-permute-done((bf16[16,2048]{1,0:T(8,128)(2,1)S(1)}, bf16[16,2048]{1,0:T(8,128)(2,1)S(1)}, u32[]{:S(2)}, u32[]{:S(2)}) %collective-permute-start.32) | collective-permute-done | bytes 65568 | tf_op jit(solution)/shard_map/ppermute | solution.py:34
  141.1 1.1 collective-permute-done.33
  142.2 0.7 fusion.7
  (55 shorter events, 1.4 us)
Async XLA Ops:
  0.6 23.4 %slice-start = ((bf16[924,2048]{1,0:T(8,128)(2,1)}), bf16[28,2048]{1,0:T(8,128)(2,1)S(1)}, s32[]{:S(2)}) async-start(bf16[924,2048]{1,0:T(8,128)(2,1)} %down_w.5), calls=%async_computation | async-start | bytes 262144 | tf_op jit(solution)/shard_map/slice | solution.py:258
  1.6 2.5 %collective-permute-start = (bf16[2,16,2048]{2,1,0:T(8,128)(2,1)S(1)}, bf16[2,16,2048]{2,1,0:T(8,128)(2,1)S(1)}, u32[]{:S(2)}, u32[]{:S(2)}) collective-permute-start(bf16[2,16,2048]{2,1,0:T(8,128)(2,1)S(1)} %get-tuple-element.97), channel_id=1, source_target_pairs={{0,1},{1,0},{2,3},{3,2},{4,5},{5,4},{6,7},{7,6},{8,9},{9,8},{10,11... | collective-permute-start | bytes 393224 | tf_op jit(solution)/shard_map/ppermute | solution.py:34
  4.1 9.6 %collective-permute-start.1 = (bf16[2,2,16,2048]{3,2,1,0:T(8,128)(2,1)S(1)}, bf16[2,2,16,2048]{3,2,1,0:T(8,128)(2,1)S(1)}, u32[]{:S(2)}, u32[]{:S(2)}) collective-permute-start(bf16[2,2,16,2048]{3,2,1,0:T(8,128)(2,1)S(1)} %get-tuple-element.92), channel_id=1, source_target_pairs={{0,2},{1,7},{2,4},{3,1},{4,6},{5,3},{6,0},{7,5},{8,10},{9,15},{10,... | collective-permute-start | bytes 786440 | tf_op jit(solution)/shard_map/ppermute | solution.py:34
  7.0 6.7 %collective-permute-start.2 = (bf16[2,16,2048]{2,1,0:T(8,128)(2,1)S(1)}, bf16[2,16,2048]{2,1,0:T(8,128)(2,1)S(1)}, u32[]{:S(2)}, u32[]{:S(2)}) collective-permute-start(bf16[2,16,2048]{2,1,0:T(8,128)(2,1)S(1)} %get-tuple-element.97), channel_id=1, source_target_pairs={{0,4},{1,5},{2,6},{3,7},{4,0},{5,1},{6,2},{7,3},{8,12},{9,13},{10,... | collective-permute-start | bytes 393224 | tf_op jit(solution)/shard_map/ppermute | solution.py:34
  13.8 4.0 %collective-permute-start.3 = (bf16[3,2,16,2048]{3,2,1,0:T(8,128)(2,1)S(1)}, bf16[3,2,16,2048]{3,2,1,0:T(8,128)(2,1)S(1)}, u32[]{:S(2)}, u32[]{:S(2)}) collective-permute-start(bf16[3,2,16,2048]{3,2,1,0:T(8,128)(2,1)S(1)} %pad_maximum_fusion.6), channel_id=1, source_target_pairs={{0,1},{1,0},{2,3},{3,2},{4,5},{5,4},{6,7},{7,6},{8,9},{9,8},{10,11... | collective-permute-start | bytes 1179656 | tf_op jit(solution)/shard_map/ppermute | solution.py:34
  17.9 16.6 %collective-permute-start.4 = (bf16[4,2,2,16,2048]{4,3,2,0,1:T(8,128)(2,1)S(1)}, bf16[4,2,2,16,2048]{4,3,2,0,1:T(8,128)(2,1)S(1)}, u32[]{:S(2)}, u32[]{:S(2)}) collective-permute-start(bf16[4,2,2,16,2048]{4,3,2,0,1:T(8,128)(2,1)S(1)} %pad_maximum_fusion.2), channel_id=1, source_target_pairs={{0,8},{1,25},{2,10},{3,27},{4,12},{5,29},{6,14},{7,31},{8,16},{9,1... | collective-permute-start | bytes 3145736 | tf_op jit(solution)/shard_map/ppermute | solution.py:34
  21.8 2.6 %copy-start = (bf16[2048,924]{0,1:T(8,128)(2,1)S(1)}, bf16[2048,924]{0,1:T(8,128)(2,1)}, u32[]{:S(2)}) copy-start(bf16[2048,924]{0,1:T(8,128)(2,1)} %param.7) | copy-start | bytes 11354116
  24.3 2.1 %copy-start.1 = (bf16[2048,924]{0,1:T(8,128)(2,1)S(1)}, bf16[2048,924]{0,1:T(8,128)(2,1)}, u32[]{:S(2)}) copy-start(bf16[2048,924]{0,1:T(8,128)(2,1)} %param.8) | copy-start | bytes 11354116
  32.0 6.4 %collective-permute-start.6 = (bf16[32,2816]{1,0:T(8,128)(2,1)S(1)}, bf16[32,2816]{1,0:T(8,128)(2,1)S(1)}, u32[]{:S(2)}, u32[]{:S(2)}) collective-permute-start(bf16[32,2816]{1,0:T(8,128)(2,1)S(1)} %get-tuple-element.47), channel_id=1, source_target_pairs={{0,32},{1,97},{2,34},{3,99},{4,36},{5,101},{6,38},{7,103},{8,40},{... | collective-permute-start | bytes 540680 | tf_op jit(solution)/shard_map/ppermute | solution.py:34
  34.5 7.2 %collective-permute-start.5 = (bf16[32,2816]{1,0:T(8,128)(2,1)S(1)}, bf16[32,2816]{1,0:T(8,128)(2,1)S(1)}, u32[]{:S(2)}, u32[]{:S(2)}) collective-permute-start(bf16[32,2816]{1,0:T(8,128)(2,1)S(1)} %get-tuple-element.45), channel_id=1, source_target_pairs={{0,96},{1,33},{2,98},{3,35},{4,100},{5,37},{6,102},{7,39},{8,104},... | collective-permute-start | bytes 540680 | tf_op jit(solution)/shard_map/ppermute | solution.py:34
  34.5 9.7 %collective-permute-start.13 = (bf16[4,2,2,16,2048]{4,3,2,0,1:T(8,128)(2,1)S(1)}, bf16[4,2,2,16,2048]{4,3,2,0,1:T(8,128)(2,1)S(1)}, u32[]{:S(2)}, u32[]{:S(2)}) collective-permute-start(bf16[4,2,2,16,2048]{4,3,2,0,1:T(8,128)(2,1)S(1)} %collective-permute-done.4), channel_id=1, source_target_pairs={{0,1},{1,0},{2,3},{3,2},{4,5},{5,4},{6,7},{7,6},{8,9},{9,8},{10,11... | collective-permute-start | bytes 3145736 | tf_op jit(solution)/shard_map/ppermute | solution.py:34
  38.4 5.6 %collective-permute-start.7 = (bf16[32,2816]{1,0:T(8,128)(2,1)S(1)}, bf16[32,2816]{1,0:T(8,128)(2,1)S(1)}, u32[]{:S(2)}, u32[]{:S(2)}) collective-permute-start(bf16[32,2816]{1,0:T(8,128)(2,1)S(1)} %add_convert_fusion.3), channel_id=1, source_target_pairs={{0,32},{1,97},{2,34},{3,99},{4,36},{5,101},{6,38},{7,103},{8,40},{... | collective-permute-start | bytes 540680 | tf_op jit(solution)/shard_map/ppermute | solution.py:34
  41.6 13.5 %collective-permute-start.12 = (bf16[4,2,16,2048]{3,2,1,0:T(8,128)(2,1)S(1)}, bf16[4,2,16,2048]{3,2,1,0:T(8,128)(2,1)S(1)}, u32[]{:S(2)}, u32[]{:S(2)}) collective-permute-start(bf16[4,2,16,2048]{3,2,1,0:T(8,128)(2,1)S(1)} %slice_bitcast_fusion), channel_id=1, source_target_pairs={{0,16},{1,17},{2,18},{3,19},{4,20},{5,21},{6,22},{7,23},{8,24},{9,... | collective-permute-start | bytes 1572872 | tf_op jit(solution)/shard_map/ppermute | solution.py:34
  44.4 27.6 %copy-start.2 = (bf16[2048,924]{0,1:T(8,128)(2,1)S(1)}, bf16[2048,924]{0,1:T(8,128)(2,1)}, u32[]{:S(2)}) copy-start(bf16[2048,924]{0,1:T(8,128)(2,1)} %param.8) | copy-start | bytes 11354116
  51.7 8.8 %collective-permute-start.24 = (bf16[64,2816]{1,0:T(8,128)(2,1)S(1)}, bf16[64,2816]{1,0:T(8,128)(2,1)S(1)}, u32[]{:S(2)}, u32[]{:S(2)}) collective-permute-start(bf16[64,2816]{1,0:T(8,128)(2,1)S(1)} %get-tuple-element.53), channel_id=1, source_target_pairs={{0,32},{1,97},{2,34},{3,99},{4,36},{5,101},{6,38},{7,103},{8,40},{... | collective-permute-start | bytes 1081352 | tf_op jit(solution)/shard_map/ppermute | solution.py:34
  55.2 8.8 %collective-permute-start.23 = (bf16[64,2816]{1,0:T(8,128)(2,1)S(1)}, bf16[64,2816]{1,0:T(8,128)(2,1)S(1)}, u32[]{:S(2)}, u32[]{:S(2)}) collective-permute-start(bf16[64,2816]{1,0:T(8,128)(2,1)S(1)} %get-tuple-element.64), channel_id=1, source_target_pairs={{0,96},{1,33},{2,98},{3,35},{4,100},{5,37},{6,102},{7,39},{8,104},... | collective-permute-start | bytes 1081352 | tf_op jit(solution)/shard_map/ppermute | solution.py:34
  55.5 16.6 %collective-permute-start.14 = (bf16[4,2,16,2048]{3,2,1,0:T(8,128)(2,1)S(1)}, bf16[4,2,16,2048]{3,2,1,0:T(8,128)(2,1)S(1)}, u32[]{:S(2)}, u32[]{:S(2)}) collective-permute-start(bf16[4,2,16,2048]{3,2,1,0:T(8,128)(2,1)S(1)} %collective-permute-done.12.refs_0_), channel_id=1, source_target_pairs={{0,1},{1,0},{2,3},{3,2},{4,5},{5,4},{6,7},{7,6},{8,9},{9,8},{10,11... | collective-permute-start | bytes 1572872 | tf_op jit(solution)/shard_map/ppermute | solution.py:34
  60.5 7.9 %collective-permute-start.25 = (bf16[64,2816]{1,0:T(8,128)(2,1)S(1)}, bf16[64,2816]{1,0:T(8,128)(2,1)S(1)}, u32[]{:S(2)}, u32[]{:S(2)}) collective-permute-start(bf16[64,2816]{1,0:T(8,128)(2,1)S(1)} %add_convert_fusion.1), channel_id=1, source_target_pairs={{0,32},{1,97},{2,34},{3,99},{4,36},{5,101},{6,38},{7,103},{8,40},{... | collective-permute-start | bytes 1081352 | tf_op jit(solution)/shard_map/ppermute | solution.py:34
  68.7 12.0 %collective-permute-start.26 = (bf16[64,2816]{1,0:T(8,128)(2,1)S(1)}, bf16[64,2816]{1,0:T(8,128)(2,1)S(1)}, u32[]{:S(2)}, u32[]{:S(2)}) collective-permute-start(bf16[64,2816]{1,0:T(8,128)(2,1)S(1)} %activation.5.mine), channel_id=1, source_target_pairs={{0,32},{1,97},{2,34},{3,99},{4,36},{5,101},{6,38},{7,103},{8,40},{... | collective-permute-start | bytes 1081352 | tf_op jit(solution)/shard_map/ppermute | solution.py:34
  77.6 4.8 %collective-permute-start.16 = (bf16[32,2816]{1,0:T(8,128)(2,1)S(1)}, bf16[32,2816]{1,0:T(8,128)(2,1)S(1)}, u32[]{:S(2)}, u32[]{:S(2)}) collective-permute-start(bf16[32,2816]{1,0:T(8,128)(2,1)S(1)} %get-tuple-element.60), channel_id=1, source_target_pairs={{0,32},{1,97},{2,34},{3,99},{4,36},{5,101},{6,38},{7,103},{8,40},{... | collective-permute-start | bytes 540680 | tf_op jit(solution)/shard_map/ppermute | solution.py:34
  77.7 22.2 %collective-permute-start.8 = (bf16[32,2816]{1,0:T(8,128)(2,1)S(1)}, bf16[32,2816]{1,0:T(8,128)(2,1)S(1)}, u32[]{:S(2)}, u32[]{:S(2)}) collective-permute-start(bf16[32,2816]{1,0:T(8,128)(2,1)S(1)} %activation.3.mine), channel_id=1, source_target_pairs={{0,32},{1,97},{2,34},{3,99},{4,36},{5,101},{6,38},{7,103},{8,40},{... | collective-permute-start | bytes 540680 | tf_op jit(solution)/shard_map/ppermute | solution.py:34
  77.8 20.2 %collective-permute-start.15 = (bf16[32,2816]{1,0:T(8,128)(2,1)S(1)}, bf16[32,2816]{1,0:T(8,128)(2,1)S(1)}, u32[]{:S(2)}, u32[]{:S(2)}) collective-permute-start(bf16[32,2816]{1,0:T(8,128)(2,1)S(1)} %get-tuple-element.58), channel_id=1, source_target_pairs={{0,96},{1,33},{2,98},{3,35},{4,100},{5,37},{6,102},{7,39},{8,104},... | collective-permute-start | bytes 540680 | tf_op jit(solution)/shard_map/ppermute | solution.py:34
  79.2 14.1 %collective-permute-start.27 = (bf16[64,2816]{1,0:T(8,128)(2,1)S(1)}, bf16[64,2816]{1,0:T(8,128)(2,1)S(1)}, u32[]{:S(2)}, u32[]{:S(2)}) collective-permute-start(bf16[64,2816]{1,0:T(8,128)(2,1)S(1)} %activation.5.mine), channel_id=1, source_target_pairs={{0,96},{1,33},{2,98},{3,35},{4,100},{5,37},{6,102},{7,39},{8,104},... | collective-permute-start | bytes 1081352 | tf_op jit(solution)/shard_map/ppermute | solution.py:34
  80.6 13.3 %collective-permute-start.28 = (bf16[64,2816]{1,0:T(8,128)(2,1)S(1)}, bf16[64,2816]{1,0:T(8,128)(2,1)S(1)}, u32[]{:S(2)}, u32[]{:S(2)}) collective-permute-start(bf16[64,2816]{1,0:T(8,128)(2,1)S(1)} %collective-permute-done.26.behind), channel_id=1, source_target_pairs={{0,32},{1,97},{2,34},{3,99},{4,36},{5,101},{6,38},{7,103},{8,40},{... | collective-permute-start | bytes 1081352 | tf_op jit(solution)/shard_map/ppermute | solution.py:34
  82.5 15.5 %collective-permute-start.17 = (bf16[32,2816]{1,0:T(8,128)(2,1)S(1)}, bf16[32,2816]{1,0:T(8,128)(2,1)S(1)}, u32[]{:S(2)}, u32[]{:S(2)}) collective-permute-start(bf16[32,2816]{1,0:T(8,128)(2,1)S(1)} %add_convert_fusion.2), channel_id=1, source_target_pairs={{0,32},{1,97},{2,34},{3,99},{4,36},{5,101},{6,38},{7,103},{8,40},{... | collective-permute-start | bytes 540680 | tf_op jit(solution)/shard_map/ppermute | solution.py:34
  97.1 24.8 %collective-permute-start.29 = (f32[4,2,16,2048]{3,2,1,0:T(8,128)S(1)}, f32[4,2,16,2048]{3,2,1,0:T(8,128)S(1)}, u32[]{:S(2)}, u32[]{:S(2)}) collective-permute-start(f32[4,2,16,2048]{3,2,1,0:T(8,128)S(1)} %get-tuple-element.67), channel_id=1, source_target_pairs={{0,1},{1,0},{2,3},{3,2},{4,5},{5,4},{6,7},{7,6},{8,9},{9,8},{10,11... | collective-permute-start | bytes 3145736 | tf_op jit(solution)/shard_map/ppermute | solution.py:34
  98.2 4.7 %collective-permute-start.18 = (bf16[32,2816]{1,0:T(8,128)(2,1)S(1)}, bf16[32,2816]{1,0:T(8,128)(2,1)S(1)}, u32[]{:S(2)}, u32[]{:S(2)}) collective-permute-start(bf16[32,2816]{1,0:T(8,128)(2,1)S(1)} %activation.4.mine), channel_id=1, source_target_pairs={{0,32},{1,97},{2,34},{3,99},{4,36},{5,101},{6,38},{7,103},{8,40},{... | collective-permute-start | bytes 540680 | tf_op jit(solution)/shard_map/ppermute | solution.py:34
  100.0 7.1 %collective-permute-start.9 = (bf16[32,2816]{1,0:T(8,128)(2,1)S(1)}, bf16[32,2816]{1,0:T(8,128)(2,1)S(1)}, u32[]{:S(2)}, u32[]{:S(2)}) collective-permute-start(bf16[32,2816]{1,0:T(8,128)(2,1)S(1)} %activation.3.mine), channel_id=1, source_target_pairs={{0,96},{1,33},{2,98},{3,35},{4,100},{5,37},{6,102},{7,39},{8,104},... | collective-permute-start | bytes 540680 | tf_op jit(solution)/shard_map/ppermute | solution.py:34
  100.0 7.1 %collective-permute-start.10 = (bf16[32,2816]{1,0:T(8,128)(2,1)S(1)}, bf16[32,2816]{1,0:T(8,128)(2,1)S(1)}, u32[]{:S(2)}, u32[]{:S(2)}) collective-permute-start(bf16[32,2816]{1,0:T(8,128)(2,1)S(1)} %collective-permute-done.8.behind), channel_id=1, source_target_pairs={{0,32},{1,97},{2,34},{3,99},{4,36},{5,101},{6,38},{7,103},{8,40},{... | collective-permute-start | bytes 540680 | tf_op jit(solution)/shard_map/ppermute | solution.py:34
  102.6 9.7 %collective-permute-start.19 = (bf16[32,2816]{1,0:T(8,128)(2,1)S(1)}, bf16[32,2816]{1,0:T(8,128)(2,1)S(1)}, u32[]{:S(2)}, u32[]{:S(2)}) collective-permute-start(bf16[32,2816]{1,0:T(8,128)(2,1)S(1)} %activation.4.mine), channel_id=1, source_target_pairs={{0,96},{1,33},{2,98},{3,35},{4,100},{5,37},{6,102},{7,39},{8,104},... | collective-permute-start | bytes 540680 | tf_op jit(solution)/shard_map/ppermute | solution.py:34
  102.9 9.4 %collective-permute-start.20 = (bf16[32,2816]{1,0:T(8,128)(2,1)S(1)}, bf16[32,2816]{1,0:T(8,128)(2,1)S(1)}, u32[]{:S(2)}, u32[]{:S(2)}) collective-permute-start(bf16[32,2816]{1,0:T(8,128)(2,1)S(1)} %collective-permute-done.18.behind), channel_id=1, source_target_pairs={{0,32},{1,97},{2,34},{3,99},{4,36},{5,101},{6,38},{7,103},{8,40},{... | collective-permute-start | bytes 540680 | tf_op jit(solution)/shard_map/ppermute | solution.py:34
  109.1 25.3 %collective-permute-start.11 = (f32[4,16,2048]{2,1,0:T(8,128)S(1)}, f32[4,16,2048]{2,1,0:T(8,128)S(1)}, u32[]{:S(2)}, u32[]{:S(2)}) collective-permute-start(f32[4,16,2048]{2,1,0:T(8,128)S(1)} %get-tuple-element.49), channel_id=1, source_target_pairs={{0,1},{1,0},{2,3},{3,2},{4,5},{5,4},{6,7},{7,6},{8,9},{9,8},{10,11... | collective-permute-start | bytes 1572872 | tf_op jit(solution)/shard_map/ppermute | solution.py:34
  114.3 2.0 %collective-permute-start.21 = (f32[4,16,2048]{2,1,0:T(8,128)S(1)}, f32[4,16,2048]{2,1,0:T(8,128)S(1)}, u32[]{:S(2)}, u32[]{:S(2)}) collective-permute-start(f32[4,16,2048]{2,1,0:T(8,128)S(1)} %get-tuple-element.62), channel_id=1, source_target_pairs={{0,1},{1,0},{2,3},{3,2},{4,5},{5,4},{6,7},{7,6},{8,9},{9,8},{10,11... | collective-permute-start | bytes 1572872 | tf_op jit(solution)/shard_map/ppermute | solution.py:34
  116.3 18.0 %collective-permute-start.22 = (bf16[4,16,2048]{2,1,0:T(8,128)(2,1)S(1)}, bf16[4,16,2048]{2,1,0:T(8,128)(2,1)S(1)}, u32[]{:S(2)}, u32[]{:S(2)}) collective-permute-start(bf16[4,16,2048]{2,1,0:T(8,128)(2,1)S(1)} %add.72), channel_id=1, source_target_pairs={{0,16},{1,17},{2,18},{3,19},{4,20},{5,21},{6,22},{7,23},{8,24},{9,... | collective-permute-start | bytes 786440 | tf_op jit(solution)/shard_map/ppermute | solution.py:34
  122.1 12.0 %collective-permute-start.30 = (bf16[4,2,16,2048]{3,2,1,0:T(8,128)(2,1)S(1)}, bf16[4,2,16,2048]{3,2,1,0:T(8,128)(2,1)S(1)}, u32[]{:S(2)}, u32[]{:S(2)}) collective-permute-start(bf16[4,2,16,2048]{3,2,1,0:T(8,128)(2,1)S(1)} %add_convert_fusion), channel_id=1, source_target_pairs={{0,24},{1,9},{2,26},{3,11},{4,28},{5,13},{6,30},{7,15},{8,0},{9,17... | collective-permute-start | bytes 1572872 | tf_op jit(solution)/shard_map/ppermute | solution.py:34
  134.2 1.6 %collective-permute-start.31 = (bf16[4,16,2048]{2,1,0:T(8,128)(2,1)S(1)}, bf16[4,16,2048]{2,1,0:T(8,128)(2,1)S(1)}, u32[]{:S(2)}, u32[]{:S(2)}) collective-permute-start(bf16[4,16,2048]{2,1,0:T(8,128)(2,1)S(1)} %pad_maximum_fusion.8), channel_id=1, source_target_pairs={{0,1},{1,0},{2,3},{3,2},{4,5},{5,4},{6,7},{7,6},{8,9},{9,8},{10,11... | collective-permute-start | bytes 786440 | tf_op jit(solution)/shard_map/ppermute | solution.py:34
  136.0 5.1 %collective-permute-start.32 = (bf16[16,2048]{1,0:T(8,128)(2,1)S(1)}, bf16[16,2048]{1,0:T(8,128)(2,1)S(1)}, u32[]{:S(2)}, u32[]{:S(2)}) collective-permute-start(bf16[16,2048]{1,0:T(8,128)(2,1)S(1)} %get-tuple-element.88), channel_id=1, source_target_pairs={{0,6},{1,3},{2,0},{3,5},{4,2},{5,7},{6,4},{7,1},{8,14},{9,11},{10,... | collective-permute-start | bytes 196616 | tf_op jit(solution)/shard_map/ppermute | solution.py:34
  136.1 5.0 %collective-permute-start.34 = (bf16[16,2048]{1,0:T(8,128)(2,1)S(1)}, bf16[16,2048]{1,0:T(8,128)(2,1)S(1)}, u32[]{:S(2)}, u32[]{:S(2)}) collective-permute-start(bf16[16,2048]{1,0:T(8,128)(2,1)S(1)} %get-tuple-element.89), channel_id=1, source_target_pairs={{0,4},{1,5},{2,6},{3,7},{4,0},{5,1},{6,2},{7,3},{8,12},{9,13},{10,... | collective-permute-start | bytes 196616 | tf_op jit(solution)/shard_map/ppermute | solution.py:34
  137.6 4.5 %collective-permute-start.33 = (bf16[16,2048]{1,0:T(8,128)(2,1)S(1)}, bf16[16,2048]{1,0:T(8,128)(2,1)S(1)}, u32[]{:S(2)}, u32[]{:S(2)}) collective-permute-start(bf16[16,2048]{1,0:T(8,128)(2,1)S(1)} %get-tuple-element.90), channel_id=1, source_target_pairs={{0,2},{1,7},{2,4},{3,1},{4,6},{5,3},{6,0},{7,5},{8,10},{9,15},{10,... | collective-permute-start | bytes 196616 | tf_op jit(solution)/shard_map/ppermute | solution.py:34

commit v3 on v2

--- a/solution.py
+++ b/solution.py
@@ -63,9 +63,13 @@
     return lax.dot_general(left, right, (dims, ((), ())), preferred_element_type=F32)
 
 
-def forward_kernel(layout, count, at, gate_w, up_w, down_w, tail_x, tail_g, *refs):
+def forward_kernel(layout, count, at, gate_w, up_w, down_w, *refs):
     sources, refs = refs[: layout[0]], refs[layout[0] :]
-    x_ref, g_ref, far, near, relay, own, part = refs
+    x_ref, g_ref, far, near, relay, own, part, tail_x, tail_g = refs
+    tail_x[...] = jnp.zeros_like(tail_x)
+    tail_g[...] = jnp.zeros_like(tail_g)
+    for i, (tail, w) in enumerate(((tail_x, gate_w), (tail_x, up_w), (tail_g, down_w))):
+        tail[i * STEP : i * STEP + TAIL] = w[MAIN:]
     for row, (source, index) in enumerate(layout[1]):
         x_ref[row * 16 : row * 16 + 16] = sources[source][(*index, 0)]
         g_ref[row * 16 : row * 16 + 16] = sources[source][(*index, 1)]
@@ -82,20 +86,20 @@
     far[...] = part[at[3]].astype(BF16)
 
 
-def forward(at, weights, tails, sources, layout):
+def forward(at, weights, sources, layout):
     rows = len(layout) * 16
-    count, depth = rows // 4, tails[0].shape[1]
+    count, depth = rows // 4, weights[2].shape[1]
     kernel = functools.partial(forward_kernel, (len(sources), layout), count)
     return call(
         kernel,
         [((rows, depth), BF16)] * 2
         + [((count, PACKED), BF16)] * 2
         + [((count, PACKED), F32)] * 2,
-        [SMEM] + [VMEM] * (5 + len(sources)),
-        [pltpu.VMEM((4, count, PACKED), F32)],
+        [SMEM] + [VMEM] * (3 + len(sources)),
+        [pltpu.VMEM((4, count, PACKED), F32)] + [pltpu.VMEM((LANES, depth), BF16)] * 2,
         (6 * rows * depth * (MAIN + TAIL), 6 * MAIN * depth),
         "forward_products",
-    )(at, *weights, tails[0], tails[1], *sources)
+    )(at, *weights, *sources)
 
 
 def swiglu_backward(gate, upward, hid_grad):
@@ -271,7 +275,7 @@
         sources, layout = chunks.send(last)
         if last is not None:
             sources = after(sources, last)
-        s["x"], s["g"], far, near, relay, own = forward(at, weights, tails, sources, layout)
+        s["x"], s["g"], far, near, relay, own = forward(at, weights, sources, layout)
         near = send(near, x_against)
         relay = (relay + send(far, x_along).astype(F32)).astype(BF16)
         if i == 0:

time: 143 us -> 143 us (level)
  Pallas kernels: 35.6 us -> 31.4 us
  local copies, waits for them, and re-layouts: 4.6 us -> 7.86 us
    pallas_call x3, Pallas kernels: 18.4 us -> 14.2 us  [forward(): call(kernel, [((rows, depth), BF16)] * 2 + [((count, PACKED), BF16)] * 2...]
    unnamed x6 -> x10, local copies, waits for them, and re-layouts: 2.08 us -> 6.23 us
    slice x4 -> x2, local copies, waits for them, and re-layouts: 2.12 us -> 0.02 us  [local(): ends = [jnp.pad(w[MAIN:], ((0, STEP - TAIL), (0, 0))) for w in weights]]
  transfers between devices with their start and end apart: 35 -> 35, of which waited for: 17 -> 17; matrix products, arithmetic and copies ran while one was open for 2% -> 2% of each run, Pallas kernels for 25% -> 22%
where the time goes in v3:
time: 143 us; the launch traced here: 142 us
  starting transfers between devices  56.9 us (40%)
  waiting for transfers between devices  42.3 us (30%)
  Pallas kernels  31.4 us (22%)
  local copies, waits for them, and re-layouts  7.86 us (5%)
  other arithmetic  2.88 us (2%)
    ppermute x35, starting transfers between devices, send(): return lax.ppermute(value, ('row', 'col'), pairs)  56.9 us
    ppermute x35, waiting for transfers between devices, send(): return lax.ppermute(value, ('row', 'col'), pairs)  42.3 us
    pallas_call x3, Pallas kernels, forward(): call(kernel, [((rows, depth), BF16)] * 2 + [((count, PACKED), BF16)] * 2...  14.2 us
    pallas_call x1, Pallas kernels, weight_gradients(): pl.pallas_call(functools.partial(weight_kernel, factor), grid=(depth // w...  9.41 us
    pallas_call x3, Pallas kernels, input_gradient(): call(functools.partial(input_kernel, planes), [((4, count, PACKED), BF16)...  7.15 us
    unnamed x10, local copies, waits for them, and re-layouts  6.23 us
  transfers between devices with their start and end apart: 35, of which 17 were waited for; matrix products, arithmetic and copies ran while one was open for 2% of the time, Pallas kernels for 22%

profile of v3, /device:TPU:1, one launch (start us, length us, event | category | flops | bytes accessed | tf_op | source)
XLA Modules:
  0.0 142.4 jit_solution(714579667630705441)
XLA Ops:
  0.6 0.9 fusion.12
  1.5 1.5 %collective-permute-start = (bf16[2,16,2048]{2,1,0:T(8,128)(2,1)S(1)}, bf16[2,16,2048]{2,1,0:T(8,128)(2,1)S(1)}, u32[]{:S(2)}, u32[]{:S(2)}) collective-permute-start(bf16[2,16,2048]{2,1,0:T(8,128)(2,1)S(1)} %get-tuple-element.94), channel_id=1, source_target_pairs={{0,1},{1,0},{2,3},{3,2},{4,5},{5,4},{6,7},{7,6},{8,9},{9,8},{10,11... | collective-permute-start | bytes 393224 | tf_op jit(solution)/shard_map/ppermute | solution.py:34
  3.0 1.0 collective-permute-done
  4.1 2.9 %collective-permute-start.1 = (bf16[2,2,16,2048]{3,2,1,0:T(8,128)(2,1)S(1)}, bf16[2,2,16,2048]{3,2,1,0:T(8,128)(2,1)S(1)}, u32[]{:S(2)}, u32[]{:S(2)}) collective-permute-start(bf16[2,2,16,2048]{3,2,1,0:T(8,128)(2,1)S(1)} %get-tuple-element.92), channel_id=1, source_target_pairs={{0,2},{1,7},{2,4},{3,1},{4,6},{5,3},{6,0},{7,5},{8,10},{9,15},{10,... | collective-permute-start | bytes 786440 | tf_op jit(solution)/shard_map/ppermute | solution.py:34
  6.9 0.3 collective-permute-start.2
  7.3 6.4 %collective-permute-done.2 = bf16[2,16,2048]{2,1,0:T(8,128)(2,1)S(1)} collective-permute-done((bf16[2,16,2048]{2,1,0:T(8,128)(2,1)S(1)}, bf16[2,16,2048]{2,1,0:T(8,128)(2,1)S(1)}, u32[]{:S(2)}, u32[]{:S(2)}) %collective-permute-start.2) | collective-permute-done | bytes 131104 | tf_op jit(solution)/shard_map/ppermute | solution.py:34
  13.7 2.6 %collective-permute-start.3 = (bf16[3,2,16,2048]{3,2,1,0:T(8,128)(2,1)S(1)}, bf16[3,2,16,2048]{3,2,1,0:T(8,128)(2,1)S(1)}, u32[]{:S(2)}, u32[]{:S(2)}) collective-permute-start(bf16[3,2,16,2048]{3,2,1,0:T(8,128)(2,1)S(1)} %pad_maximum_fusion.3), channel_id=1, source_target_pairs={{0,1},{1,0},{2,3},{3,2},{4,5},{5,4},{6,7},{7,6},{8,9},{9,8},{10,11... | collective-permute-start | bytes 1179656 | tf_op jit(solution)/shard_map/ppermute | solution.py:34
  16.3 1.3 collective-permute-done.3
  17.8 0.1 pad_maximum_fusion.2
  17.9 3.8 %collective-permute-start.4 = (bf16[4,2,2,16,2048]{4,3,2,0,1:T(8,128)(2,1)S(1)}, bf16[4,2,2,16,2048]{4,3,2,0,1:T(8,128)(2,1)}, u32[]{:S(2)}, u32[]{:S(2)}) collective-permute-start(bf16[4,2,2,16,2048]{4,3,2,0,1:T(8,128)(2,1)S(1)} %pad_maximum_fusion.2), channel_id=1, source_target_pairs={{0,8},{1,25},{2,10},{3,27},{4,12},{5,29},{6,14},{7,31},{8,16},{9,1... | collective-permute-start | bytes 3145736 | tf_op jit(solution)/shard_map/ppermute | solution.py:34
  21.9 2.1 %copy-done = bf16[2048,924]{0,1:T(8,128)(2,1)S(1)} copy-done((bf16[2048,924]{0,1:T(8,128)(2,1)S(1)}, bf16[2048,924]{0,1:T(8,128)(2,1)}, u32[]{:S(2)}) %copy-start) | copy-done | bytes 3784728
  24.0 2.1 %copy-done.2 = bf16[2048,924]{0,1:T(8,128)(2,1)S(1)} copy-done((bf16[2048,924]{0,1:T(8,128)(2,1)S(1)}, bf16[2048,924]{0,1:T(8,128)(2,1)}, u32[]{:S(2)}) %copy-start.2) | copy-done | bytes 3784728
  26.0 2.1 %copy-done.3 = bf16[924,2048]{1,0:T(8,128)(2,1)S(1)} copy-done((bf16[924,2048]{1,0:T(8,128)(2,1)S(1)}, bf16[924,2048]{1,0:T(8,128)(2,1)}, u32[]{:S(2)}) %copy-start.3) | copy-done | bytes 3784728
  28.1 4.0 %forward_products.3 = (bf16[128,2048]{1,0:T(8,128)(2,1)S(1)}, bf16[128,2048]{1,0:T(8,128)(2,1)S(1)}, bf16[32,2816]{1,0:T(8,128)(2,1)S(1)}, bf16[32,2816]{1,0:T(8...) custom-call(s32[4]{0:T(128)S(1)} %pad_add_fusion.at, bf16[924,2048]{1,0:T(8,128)(2,1)S(1)} %bitcast.62, ...), custom_call_target="tpu_custom_call" | custom-call | flops 1453326336 | bytes 11010048 | tf_op jit(solution)/shard_map/forward_products/pallas_call | solution.py:93
  32.1 2.5 %collective-permute-start.6 = (bf16[32,2816]{1,0:T(8,128)(2,1)S(1)}, bf16[32,2816]{1,0:T(8,128)(2,1)S(1)}, u32[]{:S(2)}, u32[]{:S(2)}) collective-permute-start(bf16[32,2816]{1,0:T(8,128)(2,1)S(1)} %get-tuple-element.47), channel_id=1, source_target_pairs={{0,32},{1,97},{2,34},{3,99},{4,36},{5,101},{6,38},{7,103},{8,40},{... | collective-permute-start | bytes 540680 | tf_op jit(solution)/shard_map/ppermute | solution.py:34
  34.7 0.6 collective-permute-start.13
  35.3 3.3 %collective-permute-done.6 = bf16[32,2816]{1,0:T(8,128)(2,1)S(1)} collective-permute-done((bf16[32,2816]{1,0:T(8,128)(2,1)S(1)}, bf16[32,2816]{1,0:T(8,128)(2,1)S(1)}, u32[]{:S(2)}, u32[]{:S(2)}) %collective-permute-start.6) | collective-permute-done | bytes 180256 | tf_op jit(solution)/shard_map/ppermute | solution.py:34
  38.6 3.2 %collective-permute-start.7 = (bf16[32,2816]{1,0:T(8,128)(2,1)S(1)}, bf16[32,2816]{1,0:T(8,128)(2,1)S(1)}, u32[]{:S(2)}, u32[]{:S(2)}) collective-permute-start(bf16[32,2816]{1,0:T(8,128)(2,1)S(1)} %add_convert_fusion.3), channel_id=1, source_target_pairs={{0,32},{1,97},{2,34},{3,99},{4,36},{5,101},{6,38},{7,103},{8,40},{... | collective-permute-start | bytes 540680 | tf_op jit(solution)/shard_map/ppermute | solution.py:34
  41.9 2.3 %collective-permute-done.7.relay = bf16[32,2816]{1,0:T(8,128)(2,1)S(1)} collective-permute-done((bf16[32,2816]{1,0:T(8,128)(2,1)S(1)}, bf16[32,2816]{1,0:T(8,128)(2,1)S(1)}, u32[]{:S(2)}, u32[]{:S(2)}) %collective-permute-start.7) | collective-permute-done | bytes 180256 | tf_op jit(solution)/shard_map/ppermute | solution.py:34
  44.2 0.2 activation.3.mine
  44.4 1.3 copy.13.refs_0_
  45.9 6.1 %forward_products.4 = (bf16[256,2048]{1,0:T(8,128)(2,1)S(1)}, bf16[256,2048]{1,0:T(8,128)(2,1)S(1)}, bf16[64,2816]{1,0:T(8,128)(2,1)S(1)}, bf16[64,2816]{1,0:T(8...) custom-call(s32[4]{0:T(128)S(1)} %pad_add_fusion.at, bf16[924,2048]{1,0:T(8,128)(2,1)S(1)} %bitcast.63, ...), custom_call_target="tpu_custom_call" | custom-call | flops 2906652672 | bytes 11010048 | tf_op jit(solution)/shard_map/forward_products/pallas_call | solution.py:93
  52.0 3.5 %collective-permute-start.24 = (bf16[64,2816]{1,0:T(8,128)(2,1)S(1)}, bf16[64,2816]{1,0:T(8,128)(2,1)S(1)}, u32[]{:S(2)}, u32[]{:S(2)}) collective-permute-start(bf16[64,2816]{1,0:T(8,128)(2,1)S(1)} %get-tuple-element.53), channel_id=1, source_target_pairs={{0,32},{1,97},{2,34},{3,99},{4,36},{5,101},{6,38},{7,103},{8,40},{... | collective-permute-start | bytes 1081352 | tf_op jit(solution)/shard_map/ppermute | solution.py:34
  55.5 0.2 collective-permute-start.23
  55.6 2.4 %collective-permute-start.14 = (bf16[4,2,16,2048]{3,2,1,0:T(8,128)(2,1)S(1)}, bf16[4,2,16,2048]{3,2,1,0:T(8,128)(2,1)S(1)}, u32[]{:S(2)}, u32[]{:S(2)}) collective-permute-start(bf16[4,2,16,2048]{3,2,1,0:T(8,128)(2,1)S(1)} %collective-permute-done.12.refs_0_), channel_id=1, source_target_pairs={{0,1},{1,0},{2,3},{3,2},{4,5},{5,4},{6,7},{7,6},{8,9},{9,8},{10,11... | collective-permute-start | bytes 1572872 | tf_op jit(solution)/shard_map/ppermute | solution.py:34
  58.0 2.9 %collective-permute-done.24 = bf16[64,2816]{1,0:T(8,128)(2,1)S(1)} collective-permute-done((bf16[64,2816]{1,0:T(8,128)(2,1)S(1)}, bf16[64,2816]{1,0:T(8,128)(2,1)S(1)}, u32[]{:S(2)}, u32[]{:S(2)}) %collective-permute-start.24) | collective-permute-done | bytes 360480 | tf_op jit(solution)/shard_map/ppermute | solution.py:34
  61.0 3.5 %collective-permute-start.25 = (bf16[64,2816]{1,0:T(8,128)(2,1)S(1)}, bf16[64,2816]{1,0:T(8,128)(2,1)S(1)}, u32[]{:S(2)}, u32[]{:S(2)}) collective-permute-start(bf16[64,2816]{1,0:T(8,128)(2,1)S(1)} %add_convert_fusion.1), channel_id=1, source_target_pairs={{0,32},{1,97},{2,34},{3,99},{4,36},{5,101},{6,38},{7,103},{8,40},{... | collective-permute-start | bytes 1081352 | tf_op jit(solution)/shard_map/ppermute | solution.py:34
  64.5 4.3 %collective-permute-done.25.relay = bf16[64,2816]{1,0:T(8,128)(2,1)S(1)} collective-permute-done((bf16[64,2816]{1,0:T(8,128)(2,1)S(1)}, bf16[64,2816]{1,0:T(8,128)(2,1)S(1)}, u32[]{:S(2)}, u32[]{:S(2)}) %collective-permute-start.25) | collective-permute-done | bytes 360480 | tf_op jit(solution)/shard_map/ppermute | solution.py:34
  68.8 0.3 activation.5.mine
  69.1 3.4 %collective-permute-start.26 = (bf16[64,2816]{1,0:T(8,128)(2,1)S(1)}, bf16[64,2816]{1,0:T(8,128)(2,1)S(1)}, u32[]{:S(2)}, u32[]{:S(2)}) collective-permute-start(bf16[64,2816]{1,0:T(8,128)(2,1)S(1)} %activation.5.mine), channel_id=1, source_target_pairs={{0,32},{1,97},{2,34},{3,99},{4,36},{5,101},{6,38},{7,103},{8,40},{... | collective-permute-start | bytes 1081352 | tf_op jit(solution)/shard_map/ppermute | solution.py:34
  72.5 4.0 %forward_products.5 = (bf16[128,2048]{1,0:T(8,128)(2,1)S(1)}, bf16[128,2048]{1,0:T(8,128)(2,1)S(1)}, bf16[32,2816]{1,0:T(8,128)(2,1)S(1)}, bf16[32,2816]{1,0:T(8...) custom-call(s32[4]{0:T(128)S(1)} %pad_add_fusion.at, bf16[924,2048]{1,0:T(8,128)(2,1)S(1)} %bitcast.65, ...), custom_call_target="tpu_custom_call" | custom-call | flops 1453326336 | bytes 11010048 | tf_op jit(solution)/shard_map/forward_products/pallas_call | solution.py:93
  76.8 1.5 %collective-permute-start.15 = (bf16[32,2816]{1,0:T(8,128)(2,1)S(1)}, bf16[32,2816]{1,0:T(8,128)(2,1)S(1)}, u32[]{:S(2)}, u32[]{:S(2)}) collective-permute-start(bf16[32,2816]{1,0:T(8,128)(2,1)S(1)} %get-tuple-element.58), channel_id=1, source_target_pairs={{0,96},{1,33},{2,98},{3,35},{4,100},{5,37},{6,102},{7,39},{8,104},... | collective-permute-start | bytes 540680 | tf_op jit(solution)/shard_map/ppermute | solution.py:34
  78.3 1.4 collective-permute-start.27
  79.7 1.3 collective-permute-start.28
  81.0 0.4 collective-permute-done.16
  81.4 0.9 collective-permute-start.17
  82.3 10.1 %collective-permute-done.27.ahead = bf16[64,2816]{1,0:T(8,128)(2,1)S(1)} collective-permute-done((bf16[64,2816]{1,0:T(8,128)(2,1)S(1)}, bf16[64,2816]{1,0:T(8,128)(2,1)S(1)}, u32[]{:S(2)}, u32[]{:S(2)}) %collective-permute-start.27) | collective-permute-done | bytes 360480 | tf_op jit(solution)/shard_map/ppermute | solution.py:34
  92.4 0.4 collective-permute-done.28.across
  92.8 3.2 %input_products.5 = (bf16[4,64,2816]{2,1,0:T(8,128)(2,1)S(1)}, f32[4,2,16,2048]{3,2,1,0:T(8,128)S(1)}, f32[4,2,16,2048]{3,2,1,0:T(8,128)S(1)}) custom-call(s32[4]{0:T(128)S(1)} %pad_add_fusion.at, bf16[924,2048]{1,0:T(8,128)(2,1)S(1)} %bitcast.66, bf16[924,2048]{1,0:T(8,128)(2,1)S(1)} %bitcast.73, bf16[128,2048]{1,0:T(8,128)(2,1)S(1)} %fusion.5.tail, ...), custom_call_target="tpu_custom_call" | custom-call | flops 1937768448 | bytes 7340032 | tf_op jit(solution)/shard_map/input_products/pallas_call | solution.py:175
  96.0 0.7 collective-permute-start.29
  96.7 0.2 activation.4.mine
  96.9 1.8 %collective-permute-start.18 = (bf16[32,2816]{1,0:T(8,128)(2,1)S(1)}, bf16[32,2816]{1,0:T(8,128)(2,1)S(1)}, u32[]{:S(2)}, u32[]{:S(2)}) collective-permute-start(bf16[32,2816]{1,0:T(8,128)(2,1)S(1)} %activation.4.mine), channel_id=1, source_target_pairs={{0,32},{1,97},{2,34},{3,99},{4,36},{5,101},{6,38},{7,103},{8,40},{... | collective-permute-start | bytes 540680 | tf_op jit(solution)/shard_map/ppermute | solution.py:34
  98.7 2.7 %collective-permute-start.10 = (bf16[32,2816]{1,0:T(8,128)(2,1)S(1)}, bf16[32,2816]{1,0:T(8,128)(2,1)S(1)}, u32[]{:S(2)}, u32[]{:S(2)}) collective-permute-start(bf16[32,2816]{1,0:T(8,128)(2,1)S(1)} %collective-permute-done.8.behind), channel_id=1, source_target_pairs={{0,32},{1,97},{2,34},{3,99},{4,36},{5,101},{6,38},{7,103},{8,40},{... | collective-permute-start | bytes 540680 | tf_op jit(solution)/shard_map/ppermute | solution.py:34
  101.4 0.2 collective-permute-done.18.behind
  101.6 3.1 %collective-permute-start.20 = (bf16[32,2816]{1,0:T(8,128)(2,1)S(1)}, bf16[32,2816]{1,0:T(8,128)(2,1)S(1)}, u32[]{:S(2)}, u32[]{:S(2)}) collective-permute-start(bf16[32,2816]{1,0:T(8,128)(2,1)S(1)} %collective-permute-done.18.behind), channel_id=1, source_target_pairs={{0,32},{1,97},{2,34},{3,99},{4,36},{5,101},{6,38},{7,103},{8,40},{... | collective-permute-start | bytes 540680 | tf_op jit(solution)/shard_map/ppermute | solution.py:34
  104.7 1.1 collective-permute-done.9.ahead
  105.8 2.0 %input_products.3 = (bf16[4,32,2816]{2,1,0:T(8,128)(2,1)S(1)}, f32[4,16,2048]{2,1,0:T(8,128)S(1)}, f32[4,16,2048]{2,1,0:T(8,128)S(1)}) custom-call(s32[4]{0:T(128)S(1)} %pad_add_fusion.at, bf16[924,2048]{1,0:T(8,128)(2,1)S(1)} %bitcast.67, bf16[924,2048]{1,0:T(8,128)(2,1)S(1)} %bitcast.74, bf16[128,2048]{1,0:T(8,128)(2,1)S(1)} %fusion.5.tail, ...), custom_call_target="tpu_custom_call" | custom-call | flops 968884224 | bytes 7340032 | tf_op jit(solution)/shard_map/input_products/pallas_call | solution.py:175
  107.8 3.2 %collective-permute-start.11 = (f32[4,16,2048]{2,1,0:T(8,128)S(1)}, f32[4,16,2048]{2,1,0:T(8,128)S(1)}, u32[]{:S(2)}, u32[]{:S(2)}) collective-permute-start(f32[4,16,2048]{2,1,0:T(8,128)S(1)} %get-tuple-element.49), channel_id=1, source_target_pairs={{0,1},{1,0},{2,3},{3,2},{4,5},{5,4},{6,7},{7,6},{8,9},{9,8},{10,11... | collective-permute-start | bytes 1572872 | tf_op jit(solution)/shard_map/ppermute | solution.py:34
  111.0 2.0 %input_products.4 = (bf16[4,32,2816]{2,1,0:T(8,128)(2,1)S(1)}, f32[4,16,2048]{2,1,0:T(8,128)S(1)}, f32[4,16,2048]{2,1,0:T(8,128)S(1)}) custom-call(s32[4]{0:T(128)S(1)} %pad_add_fusion.at, bf16[924,2048]{1,0:T(8,128)(2,1)S(1)} %bitcast.68, bf16[924,2048]{1,0:T(8,128)(2,1)S(1)} %bitcast.75, bf16[128,2048]{1,0:T(8,128)(2,1)S(1)} %fusion.5.tail, ...), custom_call_target="tpu_custom_call" | custom-call | flops 968884224 | bytes 7340032 | tf_op jit(solution)/shard_map/input_products/pallas_call | solution.py:175
  113.0 0.7 collective-permute-start.21
  113.7 0.2 pad_maximum_fusion.x
  113.9 0.2 pad_maximum_fusion.1.g
  114.2 1.0 collective-permute-done.21
  115.3 6.2 %collective-permute-start.22 = (bf16[4,16,2048]{2,1,0:T(8,128)(2,1)S(1)}, bf16[4,16,2048]{2,1,0:T(8,128)(2,1)S(1)}, u32[]{:S(2)}, u32[]{:S(2)}) collective-permute-start(bf16[4,16,2048]{2,1,0:T(8,128)(2,1)S(1)} %add.70), channel_id=1, source_target_pairs={{0,16},{1,17},{2,18},{3,19},{4,20},{5,21},{6,22},{7,23},{8,24},{9,... | collective-permute-start | bytes 786440 | tf_op jit(solution)/shard_map/ppermute | solution.py:34
  121.5 0.1 add_convert_fusion
  121.7 9.4 %weight_products.1 = (bf16[924,2048]{1,0:T(8,128)(2,1)}, bf16[924,2048]{1,0:T(8,128)(2,1)}, bf16[924,2048]{1,0:T(8,128)(2,1)}) custom-call(bf16[512,2048]{1,0:T(8,128)(2,1)S(1)} %pad_maximum_fusion.x, bf16[512,2048]{1,0:T(8,128)(2,1)S(1)} %pad_maximum_fusion.1.g, bf16[128,2816]{1,0:T(8,128)(2,1)S(1)} %bitcast.77, bf16[256,2816]{1,0:T(8,128)(2,1)S(1)} %bitcast.76, ...), custom_call_target="tpu_custom_call" | custom-call | flops 5813305344 | bytes 11010048 | tf_op jit(solution)/shard_map/weight_products/pallas_call | solution.py:210
  131.1 2.6 %collective-permute-done.30 = bf16[4,2,16,2048]{3,2,1,0:T(8,128)(2,1)S(1)} collective-permute-done((bf16[4,2,16,2048]{3,2,1,0:T(8,128)(2,1)S(1)}, bf16[4,2,16,2048]{3,2,1,0:T(8,128)(2,1)S(1)}, u32[]{:S(2)}, u32[]{:S(2)}) %collective-permute-start.30) | collective-permute-done | bytes 524320 | tf_op jit(solution)/shard_map/ppermute | solution.py:34
  133.8 1.5 %collective-permute-done.31 = bf16[4,16,2048]{2,1,0:T(8,128)(2,1)S(1)} collective-permute-done((bf16[4,16,2048]{2,1,0:T(8,128)(2,1)S(1)}, bf16[4,16,2048]{2,1,0:T(8,128)(2,1)S(1)}, u32[]{:S(2)}, u32[]{:S(2)}) %collective-permute-start.31) | collective-permute-done | bytes 262176 | tf_op jit(solution)/shard_map/ppermute | solution.py:34
  135.3 0.1 fusion.14
  135.6 1.2 collective-permute-start.34
  136.8 1.5 %collective-permute-start.33 = (bf16[16,2048]{1,0:T(8,128)(2,1)S(1)}, bf16[16,2048]{1,0:T(8,128)(2,1)S(1)}, u32[]{:S(2)}, u32[]{:S(2)}) collective-permute-start(bf16[16,2048]{1,0:T(8,128)(2,1)S(1)} %get-tuple-element.90), channel_id=1, source_target_pairs={{0,2},{1,7},{2,4},{3,1},{4,6},{5,3},{6,0},{7,5},{8,10},{9,15},{10,... | collective-permute-start | bytes 196616 | tf_op jit(solution)/shard_map/ppermute | solution.py:34
  138.3 3.1 %collective-permute-done.32 = bf16[16,2048]{1,0:T(8,128)(2,1)S(1)} collective-permute-done((bf16[16,2048]{1,0:T(8,128)(2,1)S(1)}, bf16[16,2048]{1,0:T(8,128)(2,1)S(1)}, u32[]{:S(2)}, u32[]{:S(2)}) %collective-permute-start.32) | collective-permute-done | bytes 65568 | tf_op jit(solution)/shard_map/ppermute | solution.py:34
  141.4 0.3 collective-permute-done.33
  141.7 0.7 fusion.11
  (54 shorter events, 1.3 us)
Async XLA Ops:
  1.5 2.5 %collective-permute-start = (bf16[2,16,2048]{2,1,0:T(8,128)(2,1)S(1)}, bf16[2,16,2048]{2,1,0:T(8,128)(2,1)S(1)}, u32[]{:S(2)}, u32[]{:S(2)}) collective-permute-start(bf16[2,16,2048]{2,1,0:T(8,128)(2,1)S(1)} %get-tuple-element.94), channel_id=1, source_target_pairs={{0,1},{1,0},{2,3},{3,2},{4,5},{5,4},{6,7},{7,6},{8,9},{9,8},{10,11... | collective-permute-start | bytes 393224 | tf_op jit(solution)/shard_map/ppermute | solution.py:34
  4.1 9.6 %collective-permute-start.1 = (bf16[2,2,16,2048]{3,2,1,0:T(8,128)(2,1)S(1)}, bf16[2,2,16,2048]{3,2,1,0:T(8,128)(2,1)S(1)}, u32[]{:S(2)}, u32[]{:S(2)}) collective-permute-start(bf16[2,2,16,2048]{3,2,1,0:T(8,128)(2,1)S(1)} %get-tuple-element.92), channel_id=1, source_target_pairs={{0,2},{1,7},{2,4},{3,1},{4,6},{5,3},{6,0},{7,5},{8,10},{9,15},{10,... | collective-permute-start | bytes 786440 | tf_op jit(solution)/shard_map/ppermute | solution.py:34
  6.9 6.7 %collective-permute-start.2 = (bf16[2,16,2048]{2,1,0:T(8,128)(2,1)S(1)}, bf16[2,16,2048]{2,1,0:T(8,128)(2,1)S(1)}, u32[]{:S(2)}, u32[]{:S(2)}) collective-permute-start(bf16[2,16,2048]{2,1,0:T(8,128)(2,1)S(1)} %get-tuple-element.94), channel_id=1, source_target_pairs={{0,4},{1,5},{2,6},{3,7},{4,0},{5,1},{6,2},{7,3},{8,12},{9,13},{10,... | collective-permute-start | bytes 393224 | tf_op jit(solution)/shard_map/ppermute | solution.py:34
  13.7 4.0 %collective-permute-start.3 = (bf16[3,2,16,2048]{3,2,1,0:T(8,128)(2,1)S(1)}, bf16[3,2,16,2048]{3,2,1,0:T(8,128)(2,1)S(1)}, u32[]{:S(2)}, u32[]{:S(2)}) collective-permute-start(bf16[3,2,16,2048]{3,2,1,0:T(8,128)(2,1)S(1)} %pad_maximum_fusion.3), channel_id=1, source_target_pairs={{0,1},{1,0},{2,3},{3,2},{4,5},{5,4},{6,7},{7,6},{8,9},{9,8},{10,11... | collective-permute-start | bytes 1179656 | tf_op jit(solution)/shard_map/ppermute | solution.py:34
  17.9 16.8 %collective-permute-start.4 = (bf16[4,2,2,16,2048]{4,3,2,0,1:T(8,128)(2,1)S(1)}, bf16[4,2,2,16,2048]{4,3,2,0,1:T(8,128)(2,1)}, u32[]{:S(2)}, u32[]{:S(2)}) collective-permute-start(bf16[4,2,2,16,2048]{4,3,2,0,1:T(8,128)(2,1)S(1)} %pad_maximum_fusion.2), channel_id=1, source_target_pairs={{0,8},{1,25},{2,10},{3,27},{4,12},{5,29},{6,14},{7,31},{8,16},{9,1... | collective-permute-start | bytes 3145736 | tf_op jit(solution)/shard_map/ppermute | solution.py:34
  21.9 2.1 %copy-start = (bf16[2048,924]{0,1:T(8,128)(2,1)S(1)}, bf16[2048,924]{0,1:T(8,128)(2,1)}, u32[]{:S(2)}) copy-start(bf16[2048,924]{0,1:T(8,128)(2,1)} %param.7) | copy-start | bytes 11354116
  24.0 2.1 %copy-start.2 = (bf16[2048,924]{0,1:T(8,128)(2,1)S(1)}, bf16[2048,924]{0,1:T(8,128)(2,1)}, u32[]{:S(2)}) copy-start(bf16[2048,924]{0,1:T(8,128)(2,1)} %param.8) | copy-start | bytes 11354116
  26.0 2.1 %copy-start.3 = (bf16[924,2048]{1,0:T(8,128)(2,1)S(1)}, bf16[924,2048]{1,0:T(8,128)(2,1)}, u32[]{:S(2)}) copy-start(bf16[924,2048]{1,0:T(8,128)(2,1)} %down_w.5) | copy-start | bytes 11354116
  32.1 13.7 %copy-start.1 = (bf16[2048,924]{0,1:T(8,128)(2,1)S(1)}, bf16[2048,924]{0,1:T(8,128)(2,1)}, u32[]{:S(2)}) copy-start(bf16[2048,924]{0,1:T(8,128)(2,1)} %param.7) | copy-start | bytes 11354116
  32.1 6.4 %collective-permute-start.6 = (bf16[32,2816]{1,0:T(8,128)(2,1)S(1)}, bf16[32,2816]{1,0:T(8,128)(2,1)S(1)}, u32[]{:S(2)}, u32[]{:S(2)}) collective-permute-start(bf16[32,2816]{1,0:T(8,128)(2,1)S(1)} %get-tuple-element.47), channel_id=1, source_target_pairs={{0,32},{1,97},{2,34},{3,99},{4,36},{5,101},{6,38},{7,103},{8,40},{... | collective-permute-start | bytes 540680 | tf_op jit(solution)/shard_map/ppermute | solution.py:34
  34.7 7.2 %collective-permute-start.5 = (bf16[32,2816]{1,0:T(8,128)(2,1)S(1)}, bf16[32,2816]{1,0:T(8,128)(2,1)S(1)}, u32[]{:S(2)}, u32[]{:S(2)}) collective-permute-start(bf16[32,2816]{1,0:T(8,128)(2,1)S(1)} %get-tuple-element.45), channel_id=1, source_target_pairs={{0,96},{1,33},{2,98},{3,35},{4,100},{5,37},{6,102},{7,39},{8,104},... | collective-permute-start | bytes 540680 | tf_op jit(solution)/shard_map/ppermute | solution.py:34
  34.7 9.7 %collective-permute-start.13 = (bf16[4,2,2,16,2048]{4,3,2,0,1:T(8,128)(2,1)}, bf16[4,2,2,16,2048]{4,3,2,0,1:T(8,128)(2,1)S(1)}, u32[]{:S(2)}, u32[]{:S(2)}) collective-permute-start(bf16[4,2,2,16,2048]{4,3,2,0,1:T(8,128)(2,1)} %collective-permute-done.4), channel_id=1, source_target_pairs={{0,1},{1,0},{2,3},{3,2},{4,5},{5,4},{6,7},{7,6},{8,9},{9,8},{10,11... | collective-permute-start | bytes 3145736 | tf_op jit(solution)/shard_map/ppermute | solution.py:34
  38.6 5.6 %collective-permute-start.7 = (bf16[32,2816]{1,0:T(8,128)(2,1)S(1)}, bf16[32,2816]{1,0:T(8,128)(2,1)S(1)}, u32[]{:S(2)}, u32[]{:S(2)}) collective-permute-start(bf16[32,2816]{1,0:T(8,128)(2,1)S(1)} %add_convert_fusion.3), channel_id=1, source_target_pairs={{0,32},{1,97},{2,34},{3,99},{4,36},{5,101},{6,38},{7,103},{8,40},{... | collective-permute-start | bytes 540680 | tf_op jit(solution)/shard_map/ppermute | solution.py:34
  41.8 13.7 %collective-permute-start.12 = (bf16[4,2,16,2048]{3,2,1,0:T(8,128)(2,1)S(1)}, bf16[4,2,16,2048]{3,2,1,0:T(8,128)(2,1)S(1)}, u32[]{:S(2)}, u32[]{:S(2)}) collective-permute-start(bf16[4,2,16,2048]{3,2,1,0:T(8,128)(2,1)S(1)} %slice_bitcast_fusion), channel_id=1, source_target_pairs={{0,16},{1,17},{2,18},{3,19},{4,20},{5,21},{6,22},{7,23},{8,24},{9,... | collective-permute-start | bytes 1572872 | tf_op jit(solution)/shard_map/ppermute | solution.py:34
  45.9 26.6 %copy-start.4 = (bf16[924,2048]{1,0:T(8,128)(2,1)S(1)}, bf16[924,2048]{1,0:T(8,128)(2,1)}, u32[]{:S(2)}) copy-start(bf16[924,2048]{1,0:T(8,128)(2,1)} %down_w.5) | copy-start | bytes 11354116
  52.0 8.9 %collective-permute-start.24 = (bf16[64,2816]{1,0:T(8,128)(2,1)S(1)}, bf16[64,2816]{1,0:T(8,128)(2,1)S(1)}, u32[]{:S(2)}, u32[]{:S(2)}) collective-permute-start(bf16[64,2816]{1,0:T(8,128)(2,1)S(1)} %get-tuple-element.53), channel_id=1, source_target_pairs={{0,32},{1,97},{2,34},{3,99},{4,36},{5,101},{6,38},{7,103},{8,40},{... | collective-permute-start | bytes 1081352 | tf_op jit(solution)/shard_map/ppermute | solution.py:34
  55.5 9.0 %collective-permute-start.23 = (bf16[64,2816]{1,0:T(8,128)(2,1)S(1)}, bf16[64,2816]{1,0:T(8,128)(2,1)S(1)}, u32[]{:S(2)}, u32[]{:S(2)}) collective-permute-start(bf16[64,2816]{1,0:T(8,128)(2,1)S(1)} %get-tuple-element.64), channel_id=1, source_target_pairs={{0,96},{1,33},{2,98},{3,35},{4,100},{5,37},{6,102},{7,39},{8,104},... | collective-permute-start | bytes 1081352 | tf_op jit(solution)/shard_map/ppermute | solution.py:34
  55.6 8.8 %collective-permute-start.14 = (bf16[4,2,16,2048]{3,2,1,0:T(8,128)(2,1)S(1)}, bf16[4,2,16,2048]{3,2,1,0:T(8,128)(2,1)S(1)}, u32[]{:S(2)}, u32[]{:S(2)}) collective-permute-start(bf16[4,2,16,2048]{3,2,1,0:T(8,128)(2,1)S(1)} %collective-permute-done.12.refs_0_), channel_id=1, source_target_pairs={{0,1},{1,0},{2,3},{3,2},{4,5},{5,4},{6,7},{7,6},{8,9},{9,8},{10,11... | collective-permute-start | bytes 1572872 | tf_op jit(solution)/shard_map/ppermute | solution.py:34
  61.0 7.9 %collective-permute-start.25 = (bf16[64,2816]{1,0:T(8,128)(2,1)S(1)}, bf16[64,2816]{1,0:T(8,128)(2,1)S(1)}, u32[]{:S(2)}, u32[]{:S(2)}) collective-permute-start(bf16[64,2816]{1,0:T(8,128)(2,1)S(1)} %add_convert_fusion.1), channel_id=1, source_target_pairs={{0,32},{1,97},{2,34},{3,99},{4,36},{5,101},{6,38},{7,103},{8,40},{... | collective-permute-start | bytes 1081352 | tf_op jit(solution)/shard_map/ppermute | solution.py:34
  69.1 10.6 %collective-permute-start.26 = (bf16[64,2816]{1,0:T(8,128)(2,1)S(1)}, bf16[64,2816]{1,0:T(8,128)(2,1)S(1)}, u32[]{:S(2)}, u32[]{:S(2)}) collective-permute-start(bf16[64,2816]{1,0:T(8,128)(2,1)S(1)} %activation.5.mine), channel_id=1, source_target_pairs={{0,32},{1,97},{2,34},{3,99},{4,36},{5,101},{6,38},{7,103},{8,40},{... | collective-permute-start | bytes 1081352 | tf_op jit(solution)/shard_map/ppermute | solution.py:34
  76.5 4.8 %collective-permute-start.16 = (bf16[32,2816]{1,0:T(8,128)(2,1)S(1)}, bf16[32,2816]{1,0:T(8,128)(2,1)S(1)}, u32[]{:S(2)}, u32[]{:S(2)}) collective-permute-start(bf16[32,2816]{1,0:T(8,128)(2,1)S(1)} %get-tuple-element.60), channel_id=1, source_target_pairs={{0,32},{1,97},{2,34},{3,99},{4,36},{5,101},{6,38},{7,103},{8,40},{... | collective-permute-start | bytes 540680 | tf_op jit(solution)/shard_map/ppermute | solution.py:34
  76.7 22.0 %collective-permute-start.8 = (bf16[32,2816]{1,0:T(8,128)(2,1)S(1)}, bf16[32,2816]{1,0:T(8,128)(2,1)S(1)}, u32[]{:S(2)}, u32[]{:S(2)}) collective-permute-start(bf16[32,2816]{1,0:T(8,128)(2,1)S(1)} %activation.3.mine), channel_id=1, source_target_pairs={{0,32},{1,97},{2,34},{3,99},{4,36},{5,101},{6,38},{7,103},{8,40},{... | collective-permute-start | bytes 540680 | tf_op jit(solution)/shard_map/ppermute | solution.py:34
  76.8 19.9 %collective-permute-start.15 = (bf16[32,2816]{1,0:T(8,128)(2,1)S(1)}, bf16[32,2816]{1,0:T(8,128)(2,1)S(1)}, u32[]{:S(2)}, u32[]{:S(2)}) collective-permute-start(bf16[32,2816]{1,0:T(8,128)(2,1)S(1)} %get-tuple-element.58), channel_id=1, source_target_pairs={{0,96},{1,33},{2,98},{3,35},{4,100},{5,37},{6,102},{7,39},{8,104},... | collective-permute-start | bytes 540680 | tf_op jit(solution)/shard_map/ppermute | solution.py:34
  78.3 14.1 %collective-permute-start.27 = (bf16[64,2816]{1,0:T(8,128)(2,1)S(1)}, bf16[64,2816]{1,0:T(8,128)(2,1)S(1)}, u32[]{:S(2)}, u32[]{:S(2)}) collective-permute-start(bf16[64,2816]{1,0:T(8,128)(2,1)S(1)} %activation.5.mine), channel_id=1, source_target_pairs={{0,96},{1,33},{2,98},{3,35},{4,100},{5,37},{6,102},{7,39},{8,104},... | collective-permute-start | bytes 1081352 | tf_op jit(solution)/shard_map/ppermute | solution.py:34
  79.7 13.2 %collective-permute-start.28 = (bf16[64,2816]{1,0:T(8,128)(2,1)S(1)}, bf16[64,2816]{1,0:T(8,128)(2,1)S(1)}, u32[]{:S(2)}, u32[]{:S(2)}) collective-permute-start(bf16[64,2816]{1,0:T(8,128)(2,1)S(1)} %collective-permute-done.26.behind), channel_id=1, source_target_pairs={{0,32},{1,97},{2,34},{3,99},{4,36},{5,101},{6,38},{7,103},{8,40},{... | collective-permute-start | bytes 1081352 | tf_op jit(solution)/shard_map/ppermute | solution.py:34
  81.4 15.3 %collective-permute-start.17 = (bf16[32,2816]{1,0:T(8,128)(2,1)S(1)}, bf16[32,2816]{1,0:T(8,128)(2,1)S(1)}, u32[]{:S(2)}, u32[]{:S(2)}) collective-permute-start(bf16[32,2816]{1,0:T(8,128)(2,1)S(1)} %add_convert_fusion.2), channel_id=1, source_target_pairs={{0,32},{1,97},{2,34},{3,99},{4,36},{5,101},{6,38},{7,103},{8,40},{... | collective-permute-start | bytes 540680 | tf_op jit(solution)/shard_map/ppermute | solution.py:34
  96.0 25.4 %collective-permute-start.29 = (f32[4,2,16,2048]{3,2,1,0:T(8,128)S(1)}, f32[4,2,16,2048]{3,2,1,0:T(8,128)S(1)}, u32[]{:S(2)}, u32[]{:S(2)}) collective-permute-start(f32[4,2,16,2048]{3,2,1,0:T(8,128)S(1)} %get-tuple-element.67), channel_id=1, source_target_pairs={{0,1},{1,0},{2,3},{3,2},{4,5},{5,4},{6,7},{7,6},{8,9},{9,8},{10,11... | collective-permute-start | bytes 3145736 | tf_op jit(solution)/shard_map/ppermute | solution.py:34
  96.9 4.7 %collective-permute-start.18 = (bf16[32,2816]{1,0:T(8,128)(2,1)S(1)}, bf16[32,2816]{1,0:T(8,128)(2,1)S(1)}, u32[]{:S(2)}, u32[]{:S(2)}) collective-permute-start(bf16[32,2816]{1,0:T(8,128)(2,1)S(1)} %activation.4.mine), channel_id=1, source_target_pairs={{0,32},{1,97},{2,34},{3,99},{4,36},{5,101},{6,38},{7,103},{8,40},{... | collective-permute-start | bytes 540680 | tf_op jit(solution)/shard_map/ppermute | solution.py:34
  98.7 7.1 %collective-permute-start.9 = (bf16[32,2816]{1,0:T(8,128)(2,1)S(1)}, bf16[32,2816]{1,0:T(8,128)(2,1)S(1)}, u32[]{:S(2)}, u32[]{:S(2)}) collective-permute-start(bf16[32,2816]{1,0:T(8,128)(2,1)S(1)} %activation.3.mine), channel_id=1, source_target_pairs={{0,96},{1,33},{2,98},{3,35},{4,100},{5,37},{6,102},{7,39},{8,104},... | collective-permute-start | bytes 540680 | tf_op jit(solution)/shard_map/ppermute | solution.py:34
  98.7 7.1 %collective-permute-start.10 = (bf16[32,2816]{1,0:T(8,128)(2,1)S(1)}, bf16[32,2816]{1,0:T(8,128)(2,1)S(1)}, u32[]{:S(2)}, u32[]{:S(2)}) collective-permute-start(bf16[32,2816]{1,0:T(8,128)(2,1)S(1)} %collective-permute-done.8.behind), channel_id=1, source_target_pairs={{0,32},{1,97},{2,34},{3,99},{4,36},{5,101},{6,38},{7,103},{8,40},{... | collective-permute-start | bytes 540680 | tf_op jit(solution)/shard_map/ppermute | solution.py:34
  101.4 9.6 %collective-permute-start.19 = (bf16[32,2816]{1,0:T(8,128)(2,1)S(1)}, bf16[32,2816]{1,0:T(8,128)(2,1)S(1)}, u32[]{:S(2)}, u32[]{:S(2)}) collective-permute-start(bf16[32,2816]{1,0:T(8,128)(2,1)S(1)} %activation.4.mine), channel_id=1, source_target_pairs={{0,96},{1,33},{2,98},{3,35},{4,100},{5,37},{6,102},{7,39},{8,104},... | collective-permute-start | bytes 540680 | tf_op jit(solution)/shard_map/ppermute | solution.py:34
  101.6 9.4 %collective-permute-start.20 = (bf16[32,2816]{1,0:T(8,128)(2,1)S(1)}, bf16[32,2816]{1,0:T(8,128)(2,1)S(1)}, u32[]{:S(2)}, u32[]{:S(2)}) collective-permute-start(bf16[32,2816]{1,0:T(8,128)(2,1)S(1)} %collective-permute-done.18.behind), channel_id=1, source_target_pairs={{0,32},{1,97},{2,34},{3,99},{4,36},{5,101},{6,38},{7,103},{8,40},{... | collective-permute-start | bytes 540680 | tf_op jit(solution)/shard_map/ppermute | solution.py:34
  107.8 26.1 %collective-permute-start.11 = (f32[4,16,2048]{2,1,0:T(8,128)S(1)}, f32[4,16,2048]{2,1,0:T(8,128)S(1)}, u32[]{:S(2)}, u32[]{:S(2)}) collective-permute-start(f32[4,16,2048]{2,1,0:T(8,128)S(1)} %get-tuple-element.49), channel_id=1, source_target_pairs={{0,1},{1,0},{2,3},{3,2},{4,5},{5,4},{6,7},{7,6},{8,9},{9,8},{10,11... | collective-permute-start | bytes 1572872 | tf_op jit(solution)/shard_map/ppermute | solution.py:34
  113.0 2.3 %collective-permute-start.21 = (f32[4,16,2048]{2,1,0:T(8,128)S(1)}, f32[4,16,2048]{2,1,0:T(8,128)S(1)}, u32[]{:S(2)}, u32[]{:S(2)}) collective-permute-start(f32[4,16,2048]{2,1,0:T(8,128)S(1)} %get-tuple-element.62), channel_id=1, source_target_pairs={{0,1},{1,0},{2,3},{3,2},{4,5},{5,4},{6,7},{7,6},{8,9},{9,8},{10,11... | collective-permute-start | bytes 1572872 | tf_op jit(solution)/shard_map/ppermute | solution.py:34
  115.3 18.5 %collective-permute-start.22 = (bf16[4,16,2048]{2,1,0:T(8,128)(2,1)S(1)}, bf16[4,16,2048]{2,1,0:T(8,128)(2,1)S(1)}, u32[]{:S(2)}, u32[]{:S(2)}) collective-permute-start(bf16[4,16,2048]{2,1,0:T(8,128)(2,1)S(1)} %add.70), channel_id=1, source_target_pairs={{0,16},{1,17},{2,18},{3,19},{4,20},{5,21},{6,22},{7,23},{8,24},{9,... | collective-permute-start | bytes 786440 | tf_op jit(solution)/shard_map/ppermute | solution.py:34
  121.6 12.1 %collective-permute-start.30 = (bf16[4,2,16,2048]{3,2,1,0:T(8,128)(2,1)S(1)}, bf16[4,2,16,2048]{3,2,1,0:T(8,128)(2,1)S(1)}, u32[]{:S(2)}, u32[]{:S(2)}) collective-permute-start(bf16[4,2,16,2048]{3,2,1,0:T(8,128)(2,1)S(1)} %add_convert_fusion), channel_id=1, source_target_pairs={{0,24},{1,9},{2,26},{3,11},{4,28},{5,13},{6,30},{7,15},{8,0},{9,17... | collective-permute-start | bytes 1572872 | tf_op jit(solution)/shard_map/ppermute | solution.py:34
  133.7 1.6 %collective-permute-start.31 = (bf16[4,16,2048]{2,1,0:T(8,128)(2,1)S(1)}, bf16[4,16,2048]{2,1,0:T(8,128)(2,1)S(1)}, u32[]{:S(2)}, u32[]{:S(2)}) collective-permute-start(bf16[4,16,2048]{2,1,0:T(8,128)(2,1)S(1)} %pad_maximum_fusion.5), channel_id=1, source_target_pairs={{0,1},{1,0},{2,3},{3,2},{4,5},{5,4},{6,7},{7,6},{8,9},{9,8},{10,11... | collective-permute-start | bytes 786440 | tf_op jit(solution)/shard_map/ppermute | solution.py:34
  135.5 5.9 %collective-permute-start.32 = (bf16[16,2048]{1,0:T(8,128)(2,1)S(1)}, bf16[16,2048]{1,0:T(8,128)(2,1)S(1)}, u32[]{:S(2)}, u32[]{:S(2)}) collective-permute-start(bf16[16,2048]{1,0:T(8,128)(2,1)S(1)} %get-tuple-element.88), channel_id=1, source_target_pairs={{0,6},{1,3},{2,0},{3,5},{4,2},{5,7},{6,4},{7,1},{8,14},{9,11},{10,... | collective-permute-start | bytes 196616 | tf_op jit(solution)/shard_map/ppermute | solution.py:34
  135.6 5.8 %collective-permute-start.34 = (bf16[16,2048]{1,0:T(8,128)(2,1)S(1)}, bf16[16,2048]{1,0:T(8,128)(2,1)S(1)}, u32[]{:S(2)}, u32[]{:S(2)}) collective-permute-start(bf16[16,2048]{1,0:T(8,128)(2,1)S(1)} %get-tuple-element.89), channel_id=1, source_target_pairs={{0,4},{1,5},{2,6},{3,7},{4,0},{5,1},{6,2},{7,3},{8,12},{9,13},{10,... | collective-permute-start | bytes 196616 | tf_op jit(solution)/shard_map/ppermute | solution.py:34
  136.8 4.9 %collective-permute-start.33 = (bf16[16,2048]{1,0:T(8,128)(2,1)S(1)}, bf16[16,2048]{1,0:T(8,128)(2,1)S(1)}, u32[]{:S(2)}, u32[]{:S(2)}) collective-permute-start(bf16[16,2048]{1,0:T(8,128)(2,1)S(1)} %get-tuple-element.90), channel_id=1, source_target_pairs={{0,2},{1,7},{2,4},{3,1},{4,6},{5,3},{6,0},{7,5},{8,10},{9,15},{10,... | collective-permute-start | bytes 196616 | tf_op jit(solution)/shard_map/ppermute | solution.py:34
